TPU v7x, 256 devices: a whole 4x4x8 slice. The times are simulated.
256 devices in a mesh: section: 4 (over z_lo, core), tile: 64 (over y, x, z_hi).
Axes of the slice: x: 4, y: 4, z: 8 (z_hi: 4, z_lo: 2; z = z_hi * 2 + z_lo), core: 2. Of those that a mesh axis runs over, the one named last changes fastest.
Arguments:
- frames: bfloat16 [3, 64, 8, 10240], P(None, 'tile'), may hold values from -6 to 6
- weights: bfloat16 [4, 3, 3, 256, 512], P('section'), may hold values from -0.75 to 0.75
- bias: bfloat16 [4, 512], P('section'), may hold values from -4 to 4
Outputs:
- hidden_seq: bfloat16 [4, 3, 64, 8, 10240], P('section', None, 'tile')
- final_cell: float32 [4, 64, 8, 10240], P('section', 'tile')
All inputs are finite; a program needn't handle non-finite values.
Results may differ from a plain program's by a relative error of at most 0.008.
Values may be sent and summed in bfloat16 or wider, within the bound.
A program may use at most 64 MiB of HBM per device.

v0:
```python
import jax
import jax.numpy as jnp
from jax import lax
from jax.sharding import PartitionSpec as P

TCOLS = 8


def shifted(value, axis, steps):
    count = lax.axis_size(axis)
    first, last = (max(0, -steps), min(count, count - steps))
    return lax.ppermute(value, axis, [(source, source + steps) for source in range(first, last)])


def add_rims(field):
    column = lax.axis_index("tile") % TCOLS
    west = shifted(field[:, :, -1:, :], "tile", 1)
    east = shifted(field[:, :, :1, :], "tile", -1)
    west = jnp.where(column == 0, jnp.zeros_like(west), west)
    east = jnp.where(column == TCOLS - 1, jnp.zeros_like(east), east)
    wide = jnp.concatenate([west, field, east], axis=2)
    north = shifted(wide[:, -1:, :, :], "tile", TCOLS)
    south = shifted(wide[:, :1, :, :], "tile", -TCOLS)
    return jnp.concatenate([north, wide, south], axis=1)


def advance(extended, cell, kernel, gate_bias, rows, cols, width):
    pieces = []
    for row_off in range(3):
        for col_off in range(3):
            pieces.append(extended[row_off : row_off + rows, col_off : col_off + cols, :])
    columns = jnp.concatenate(pieces, axis=-1).reshape(rows * cols, 18 * width)
    gates = jnp.dot(columns, kernel, preferred_element_type=jnp.float32) + gate_bias
    new_cell = jax.nn.sigmoid(gates[:, width : 2 * width]) * cell + jax.nn.sigmoid(
        gates[:, :width]
    ) * jnp.tanh(gates[:, 3 * width :])
    new_hidden = (jax.nn.sigmoid(gates[:, 2 * width : 3 * width]) * jnp.tanh(new_cell)).astype(
        jnp.bfloat16
    )
    return (new_hidden.reshape(rows, cols, width), new_cell)


def local(frames, weights, bias):
    steps_in = frames.shape[0]
    rows = frames.shape[2]
    width = bias.shape[1] // 4
    cols = frames.shape[3] // width
    frames = frames.reshape(steps_in, rows, cols, width)
    kernel = weights.reshape(18 * width, 4 * width)
    gate_bias = bias[0].astype(jnp.float32)
    section = lax.axis_index("section")
    sections = lax.axis_size("section")
    hidden = jnp.zeros((rows, cols, width), jnp.bfloat16)
    cell = jnp.zeros((rows * cols, width), jnp.float32)
    history = jnp.zeros((steps_in, rows, cols, width), jnp.bfloat16)
    waves = steps_in + sections - 1
    incoming = jnp.zeros((rows, cols, width), jnp.bfloat16)
    for wave in range(waves):
        moment = wave - section
        valid = jnp.logical_and(moment >= 0, moment < steps_in)
        spot = jnp.clip(moment, 0, steps_in - 1)
        first = min(wave, steps_in - 1)
        if wave > 0:
            incoming = shifted(hidden, "section", 1)
        source = jnp.where(section == 0, frames[first], incoming)
        extended = add_rims(jnp.concatenate([source, hidden], axis=-1)[None])[0]
        new_hidden, new_cell = advance(extended, cell, kernel, gate_bias, rows, cols, width)
        hidden = jnp.where(valid, new_hidden, hidden)
        cell = jnp.where(valid, new_cell, cell)
        zero = jnp.zeros((), jnp.int32)
        updated = lax.dynamic_update_slice(history, new_hidden[None], (spot, zero, zero, zero))
        history = jnp.where(valid, updated, history)
    hidden_seq = history.reshape(1, steps_in, 1, rows, cols * width)
    final_cell = cell.reshape(1, 1, rows, cols * width)
    return (hidden_seq, final_cell)


def solution(mesh):
    placed = (P(None, "tile", None, None), P("section", None, None, None, None), P("section", None))
    return jax.shard_map(
        local,
        mesh=mesh,
        in_specs=placed,
        out_specs=(P("section", None, "tile", None, None), P("section", "tile", None, None)),
        check_vma=False,
    )
```

profile of v0, /device:TPU:56, one launch (start us, length us, event | category | flops | bytes accessed | tf_op | source)
XLA Modules:
  0.0 205.4 jit_solution(15598231857016551793)
XLA Ops:
  2.0 9.7 %collective-permute-start.1 = (bf16[1,8,1,256]{3,2,1,0:T(2,128)(2,1)S(1)}, bf16[1,8,1,256]{3,2,1,0:T(2,128)(2,1)S(1)}, u32[]{:S(2)}, u32[]{:S(2)}) collective-permute-start(bf16[1,8,1,256]{3,2,1,0:T(2,128)(2,1)S(1)} %get-tuple-element.42), channel_id=1, source_target_pairs={{1,0},{2,1},{3,2},{4,3},{5,4},{6,5},{7,6},{8,7},{9,8},{10,9},{11,1... | collective-permute-start | bytes 12296 | tf_op jit(solution)/shard_map/ppermute | solution.py:12
  13.7 8.7 %collective-permute-done = bf16[1,8,1,256]{3,2,1,0:T(2,128)(2,1)S(1)} collective-permute-done((bf16[1,8,1,256]{3,2,1,0:T(2,128)(2,1)S(1)}, bf16[1,8,1,256]{3,2,1,0:T(2,128)(2,1)S(1)}, u32[]{:S(2)}, u32[]{:S(2)}) %collective-permute-start) | collective-permute-done | bytes 4128 | tf_op jit(solution)/shard_map/ppermute | solution.py:12
  24.3 5.4 %collective-permute-start.2 = (bf16[1,1,82,256]{3,2,1,0:T(8,128)(2,1)S(1)}, bf16[1,1,82,256]{3,2,1,0:T(8,128)(2,1)S(1)}, u32[]{:S(2)}, u32[]{:S(2)}) collective-permute-start(bf16[1,1,82,256]{3,2,1,0:T(8,128)(2,1)S(1)} %get-tuple-element.29), channel_id=1, source_target_pairs={{0,8},{1,9},{2,10},{3,11},{4,12},{5,13},{6,14},{7,15},{8,16},{9,17... | collective-permute-start | bytes 125960 | tf_op jit(solution)/shard_map/ppermute | solution.py:12
  30.5 2.2 %collective-permute-done.2 = bf16[1,1,82,256]{3,2,1,0:T(8,128)(2,1)S(1)} collective-permute-done((bf16[1,1,82,256]{3,2,1,0:T(8,128)(2,1)S(1)}, bf16[1,1,82,256]{3,2,1,0:T(8,128)(2,1)S(1)}, u32[]{:S(2)}, u32[]{:S(2)}) %collective-permute-start.2) | collective-permute-done | bytes 42016 | tf_op jit(solution)/shard_map/ppermute | solution.py:12
  37.4 4.7 %collective-permute-done.4 = bf16[8,80,128]{2,1,0:T(8,128)(2,1)S(1)} collective-permute-done((bf16[8,80,128]{2,1,0:T(8,128)(2,1)S(1)}, bf16[8,80,128]{2,1,0:T(8,128)(2,1)S(1)}, u32[]{:S(2)}, u32[]{:S(2)}) %collective-permute-start.4) | collective-permute-done | bytes 163872 | tf_op jit(solution)/shard_map/ppermute | solution.py:12
  44.2 4.8 %collective-permute-start.5 = (bf16[1,8,1,256]{3,2,1,0:T(2,128)(2,1)S(1)}, bf16[1,8,1,256]{3,2,1,0:T(2,128)(2,1)S(1)}, u32[]{:S(2)}, u32[]{:S(2)}) collective-permute-start(bf16[1,8,1,256]{3,2,1,0:T(2,128)(2,1)S(1)} %get-tuple-element.39), channel_id=1, source_target_pairs={{0,1},{1,2},{2,3},{3,4},{4,5},{5,6},{6,7},{7,8},{8,9},{9,10},{10,1... | collective-permute-start | bytes 12296 | tf_op jit(solution)/shard_map/ppermute | solution.py:12
  49.0 5.8 %collective-permute-done.5 = bf16[1,8,1,256]{3,2,1,0:T(2,128)(2,1)S(1)} collective-permute-done((bf16[1,8,1,256]{3,2,1,0:T(2,128)(2,1)S(1)}, bf16[1,8,1,256]{3,2,1,0:T(2,128)(2,1)S(1)}, u32[]{:S(2)}, u32[]{:S(2)}) %collective-permute-start.5) | collective-permute-done | bytes 4128 | tf_op jit(solution)/shard_map/ppermute | solution.py:12
  54.9 2.3 %collective-permute-start.8 = (bf16[1,1,82,256]{3,2,1,0:T(8,128)(2,1)S(1)}, bf16[1,1,82,256]{3,2,1,0:T(8,128)(2,1)S(1)}, u32[]{:S(2)}, u32[]{:S(2)}) collective-permute-start(bf16[1,1,82,256]{3,2,1,0:T(8,128)(2,1)S(1)} %get-tuple-element.28), channel_id=1, source_target_pairs={{8,0},{9,1},{10,2},{11,3},{12,4},{13,5},{14,6},{15,7},{16,8},{17,9... | collective-permute-start | bytes 125960 | tf_op jit(solution)/shard_map/ppermute | solution.py:12
  57.2 5.0 %collective-permute-start.7 = (bf16[1,1,82,256]{3,2,1,0:T(8,128)(2,1)S(1)}, bf16[1,1,82,256]{3,2,1,0:T(8,128)(2,1)S(1)}, u32[]{:S(2)}, u32[]{:S(2)}) collective-permute-start(bf16[1,1,82,256]{3,2,1,0:T(8,128)(2,1)S(1)} %get-tuple-element.27), channel_id=1, source_target_pairs={{0,8},{1,9},{2,10},{3,11},{4,12},{5,13},{6,14},{7,15},{8,16},{9,17... | collective-permute-start | bytes 125960 | tf_op jit(solution)/shard_map/ppermute | solution.py:12
  62.3 3.2 %collective-permute-done.7 = bf16[1,1,82,256]{3,2,1,0:T(8,128)(2,1)S(1)} collective-permute-done((bf16[1,1,82,256]{3,2,1,0:T(8,128)(2,1)S(1)}, bf16[1,1,82,256]{3,2,1,0:T(8,128)(2,1)S(1)}, u32[]{:S(2)}, u32[]{:S(2)}) %collective-permute-start.7) | collective-permute-done | bytes 42016 | tf_op jit(solution)/shard_map/ppermute | solution.py:12
  71.0 4.7 %collective-permute-done.9 = bf16[8,80,128]{2,1,0:T(8,128)(2,1)S(1)} collective-permute-done((bf16[8,80,128]{2,1,0:T(8,128)(2,1)S(1)}, bf16[8,80,128]{2,1,0:T(8,128)(2,1)S(1)}, u32[]{:S(2)}, u32[]{:S(2)}) %collective-permute-start.9) | collective-permute-done | bytes 163872 | tf_op jit(solution)/shard_map/ppermute | solution.py:12
  77.8 4.8 %collective-permute-start.10 = (bf16[1,8,1,256]{3,2,1,0:T(2,128)(2,1)S(1)}, bf16[1,8,1,256]{3,2,1,0:T(2,128)(2,1)S(1)}, u32[]{:S(2)}, u32[]{:S(2)}) collective-permute-start(bf16[1,8,1,256]{3,2,1,0:T(2,128)(2,1)S(1)} %get-tuple-element.37), channel_id=1, source_target_pairs={{0,1},{1,2},{2,3},{3,4},{4,5},{5,6},{6,7},{7,8},{8,9},{9,10},{10,1... | collective-permute-start | bytes 12296 | tf_op jit(solution)/shard_map/ppermute | solution.py:12
  82.6 5.8 %collective-permute-done.10 = bf16[1,8,1,256]{3,2,1,0:T(2,128)(2,1)S(1)} collective-permute-done((bf16[1,8,1,256]{3,2,1,0:T(2,128)(2,1)S(1)}, bf16[1,8,1,256]{3,2,1,0:T(2,128)(2,1)S(1)}, u32[]{:S(2)}, u32[]{:S(2)}) %collective-permute-start.10) | collective-permute-done | bytes 4128 | tf_op jit(solution)/shard_map/ppermute | solution.py:12
  91.0 6.0 %collective-permute-start.12 = (bf16[1,1,82,256]{3,2,1,0:T(8,128)(2,1)}, bf16[1,1,82,256]{3,2,1,0:T(8,128)(2,1)}, u32[]{:S(2)}, u32[]{:S(2)}) collective-permute-start(bf16[1,1,82,256]{3,2,1,0:T(8,128)(2,1)} %get-tuple-element.25), channel_id=1, source_target_pairs={{0,8},{1,9},{2,10},{3,11},{4,12},{5,13},{6,14},{7,15},{8,16},{9,17... | collective-permute-start | bytes 125960 | tf_op jit(solution)/shard_map/ppermute | solution.py:12
  97.1 2.6 %collective-permute-done.12 = bf16[1,1,82,256]{3,2,1,0:T(8,128)(2,1)} collective-permute-done((bf16[1,1,82,256]{3,2,1,0:T(8,128)(2,1)}, bf16[1,1,82,256]{3,2,1,0:T(8,128)(2,1)}, u32[]{:S(2)}, u32[]{:S(2)}) %collective-permute-start.12) | collective-permute-done | bytes 42016 | tf_op jit(solution)/shard_map/ppermute | solution.py:12
  106.0 4.7 %collective-permute-done.14 = bf16[8,80,128]{2,1,0:T(8,128)(2,1)S(1)} collective-permute-done((bf16[8,80,128]{2,1,0:T(8,128)(2,1)S(1)}, bf16[8,80,128]{2,1,0:T(8,128)(2,1)S(1)}, u32[]{:S(2)}, u32[]{:S(2)}) %collective-permute-start.14) | collective-permute-done | bytes 163872 | tf_op jit(solution)/shard_map/ppermute | solution.py:12
  112.8 4.8 %collective-permute-start.15 = (bf16[1,8,1,256]{3,2,1,0:T(2,128)(2,1)S(1)}, bf16[1,8,1,256]{3,2,1,0:T(2,128)(2,1)S(1)}, u32[]{:S(2)}, u32[]{:S(2)}) collective-permute-start(bf16[1,8,1,256]{3,2,1,0:T(2,128)(2,1)S(1)} %get-tuple-element.35), channel_id=1, source_target_pairs={{0,1},{1,2},{2,3},{3,4},{4,5},{5,6},{6,7},{7,8},{8,9},{9,10},{10,1... | collective-permute-start | bytes 12296 | tf_op jit(solution)/shard_map/ppermute | solution.py:12
  117.6 5.8 %collective-permute-done.15 = bf16[1,8,1,256]{3,2,1,0:T(2,128)(2,1)S(1)} collective-permute-done((bf16[1,8,1,256]{3,2,1,0:T(2,128)(2,1)S(1)}, bf16[1,8,1,256]{3,2,1,0:T(2,128)(2,1)S(1)}, u32[]{:S(2)}, u32[]{:S(2)}) %collective-permute-start.15) | collective-permute-done | bytes 4128 | tf_op jit(solution)/shard_map/ppermute | solution.py:12
  123.5 2.4 %collective-permute-start.18 = (bf16[1,1,82,256]{3,2,1,0:T(8,128)(2,1)S(1)}, bf16[1,1,82,256]{3,2,1,0:T(8,128)(2,1)S(1)}, u32[]{:S(2)}, u32[]{:S(2)}) collective-permute-start(bf16[1,1,82,256]{3,2,1,0:T(8,128)(2,1)S(1)} %get-tuple-element.24), channel_id=1, source_target_pairs={{8,0},{9,1},{10,2},{11,3},{12,4},{13,5},{14,6},{15,7},{16,8},{17,9... | collective-permute-start | bytes 125960 | tf_op jit(solution)/shard_map/ppermute | solution.py:12
  125.9 5.0 %collective-permute-start.17 = (bf16[1,1,82,256]{3,2,1,0:T(8,128)(2,1)S(1)}, bf16[1,1,82,256]{3,2,1,0:T(8,128)(2,1)S(1)}, u32[]{:S(2)}, u32[]{:S(2)}) collective-permute-start(bf16[1,1,82,256]{3,2,1,0:T(8,128)(2,1)S(1)} %get-tuple-element.23), channel_id=1, source_target_pairs={{0,8},{1,9},{2,10},{3,11},{4,12},{5,13},{6,14},{7,15},{8,16},{9,17... | collective-permute-start | bytes 125960 | tf_op jit(solution)/shard_map/ppermute | solution.py:12
  130.9 3.3 %collective-permute-done.17 = bf16[1,1,82,256]{3,2,1,0:T(8,128)(2,1)S(1)} collective-permute-done((bf16[1,1,82,256]{3,2,1,0:T(8,128)(2,1)S(1)}, bf16[1,1,82,256]{3,2,1,0:T(8,128)(2,1)S(1)}, u32[]{:S(2)}, u32[]{:S(2)}) %collective-permute-start.17) | collective-permute-done | bytes 42016 | tf_op jit(solution)/shard_map/ppermute | solution.py:12
  139.8 4.7 %collective-permute-done.19 = bf16[8,80,128]{2,1,0:T(8,128)(2,1)S(1)} collective-permute-done((bf16[8,80,128]{2,1,0:T(8,128)(2,1)S(1)}, bf16[8,80,128]{2,1,0:T(8,128)(2,1)S(1)}, u32[]{:S(2)}, u32[]{:S(2)}) %collective-permute-start.19) | collective-permute-done | bytes 163872 | tf_op jit(solution)/shard_map/ppermute | solution.py:12
  146.6 4.8 %collective-permute-start.20 = (bf16[1,8,1,256]{3,2,1,0:T(2,128)(2,1)S(1)}, bf16[1,8,1,256]{3,2,1,0:T(2,128)(2,1)S(1)}, u32[]{:S(2)}, u32[]{:S(2)}) collective-permute-start(bf16[1,8,1,256]{3,2,1,0:T(2,128)(2,1)S(1)} %get-tuple-element.33), channel_id=1, source_target_pairs={{0,1},{1,2},{2,3},{3,4},{4,5},{5,6},{6,7},{7,8},{8,9},{9,10},{10,1... | collective-permute-start | bytes 12296 | tf_op jit(solution)/shard_map/ppermute | solution.py:12
  151.5 5.8 %collective-permute-done.20 = bf16[1,8,1,256]{3,2,1,0:T(2,128)(2,1)S(1)} collective-permute-done((bf16[1,8,1,256]{3,2,1,0:T(2,128)(2,1)S(1)}, bf16[1,8,1,256]{3,2,1,0:T(2,128)(2,1)S(1)}, u32[]{:S(2)}, u32[]{:S(2)}) %collective-permute-start.20) | collective-permute-done | bytes 4128 | tf_op jit(solution)/shard_map/ppermute | solution.py:12
  157.3 1.9 collective-permute-start.23
  159.3 5.6 %collective-permute-start.22 = (bf16[1,1,82,256]{3,2,1,0:T(8,128)(2,1)S(1)}, bf16[1,1,82,256]{3,2,1,0:T(8,128)(2,1)S(1)}, u32[]{:S(2)}, u32[]{:S(2)}) collective-permute-start(bf16[1,1,82,256]{3,2,1,0:T(8,128)(2,1)S(1)} %get-tuple-element.21), channel_id=1, source_target_pairs={{0,8},{1,9},{2,10},{3,11},{4,12},{5,13},{6,14},{7,15},{8,16},{9,17... | collective-permute-start | bytes 125960 | tf_op jit(solution)/shard_map/ppermute | solution.py:12
  164.9 2.7 %collective-permute-done.22 = bf16[1,1,82,256]{3,2,1,0:T(8,128)(2,1)S(1)} collective-permute-done((bf16[1,1,82,256]{3,2,1,0:T(8,128)(2,1)S(1)}, bf16[1,1,82,256]{3,2,1,0:T(8,128)(2,1)S(1)}, u32[]{:S(2)}, u32[]{:S(2)}) %collective-permute-start.22) | collective-permute-done | bytes 42016 | tf_op jit(solution)/shard_map/ppermute | solution.py:12
  173.0 4.6 %collective-permute-done.24 = bf16[8,80,128]{2,1,0:T(8,128)(2,1)S(1)} collective-permute-done((bf16[8,80,128]{2,1,0:T(8,128)(2,1)S(1)}, bf16[8,80,128]{2,1,0:T(8,128)(2,1)S(1)}, u32[]{:S(2)}, u32[]{:S(2)}) %collective-permute-start.24) | collective-permute-done | bytes 163872 | tf_op jit(solution)/shard_map/ppermute | solution.py:12
  179.8 4.8 %collective-permute-start.25 = (bf16[1,8,1,256]{3,2,1,0:T(2,128)(2,1)S(1)}, bf16[1,8,1,256]{3,2,1,0:T(2,128)(2,1)S(1)}, u32[]{:S(2)}, u32[]{:S(2)}) collective-permute-start(bf16[1,8,1,256]{3,2,1,0:T(2,128)(2,1)S(1)} %get-tuple-element.31), channel_id=1, source_target_pairs={{0,1},{1,2},{2,3},{3,4},{4,5},{5,6},{6,7},{7,8},{8,9},{9,10},{10,1... | collective-permute-start | bytes 12296 | tf_op jit(solution)/shard_map/ppermute | solution.py:12
  184.6 5.8 %collective-permute-done.25 = bf16[1,8,1,256]{3,2,1,0:T(2,128)(2,1)S(1)} collective-permute-done((bf16[1,8,1,256]{3,2,1,0:T(2,128)(2,1)S(1)}, bf16[1,8,1,256]{3,2,1,0:T(2,128)(2,1)S(1)}, u32[]{:S(2)}, u32[]{:S(2)}) %collective-permute-start.25) | collective-permute-done | bytes 4128 | tf_op jit(solution)/shard_map/ppermute | solution.py:12
  192.4 5.4 %collective-permute-start.27 = (bf16[1,1,82,256]{3,2,1,0:T(8,128)(2,1)S(1)}, bf16[1,1,82,256]{3,2,1,0:T(8,128)(2,1)S(1)}, u32[]{:S(2)}, u32[]{:S(2)}) collective-permute-start(bf16[1,1,82,256]{3,2,1,0:T(8,128)(2,1)S(1)} %get-tuple-element.19), channel_id=1, source_target_pairs={{0,8},{1,9},{2,10},{3,11},{4,12},{5,13},{6,14},{7,15},{8,16},{9,17... | collective-permute-start | bytes 125960 | tf_op jit(solution)/shard_map/ppermute | solution.py:12
  197.9 2.8 %collective-permute-done.27 = bf16[1,1,82,256]{3,2,1,0:T(8,128)(2,1)S(1)} collective-permute-done((bf16[1,1,82,256]{3,2,1,0:T(8,128)(2,1)S(1)}, bf16[1,1,82,256]{3,2,1,0:T(8,128)(2,1)S(1)}, u32[]{:S(2)}, u32[]{:S(2)}) %collective-permute-start.27) | collective-permute-done | bytes 42016 | tf_op jit(solution)/shard_map/ppermute | solution.py:12
  (176 shorter events, 52.7 us)
Async XLA Ops:
  0.6 32.8 %copy-start = (bf16[1,3,3,256,512]{4,3,2,1,0:T(8,128)(2,1)S(1)}, bf16[1,3,3,256,512]{4,3,2,1,0:T(8,128)(2,1)}, u32[]{:S(2)}) copy-start(bf16[1,3,3,256,512]{4,3,2,1,0:T(8,128)(2,1)} %param.4) | copy-start | bytes 7077892
  2.0 11.6 %collective-permute-start.1 = (bf16[1,8,1,256]{3,2,1,0:T(2,128)(2,1)S(1)}, bf16[1,8,1,256]{3,2,1,0:T(2,128)(2,1)S(1)}, u32[]{:S(2)}, u32[]{:S(2)}) collective-permute-start(bf16[1,8,1,256]{3,2,1,0:T(2,128)(2,1)S(1)} %get-tuple-element.42), channel_id=1, source_target_pairs={{1,0},{2,1},{3,2},{4,3},{5,4},{6,5},{7,6},{8,7},{9,8},{10,9},{11,1... | collective-permute-start | bytes 12296 | tf_op jit(solution)/shard_map/ppermute | solution.py:12
  11.7 10.7 %collective-permute-start = (bf16[1,8,1,256]{3,2,1,0:T(2,128)(2,1)S(1)}, bf16[1,8,1,256]{3,2,1,0:T(2,128)(2,1)S(1)}, u32[]{:S(2)}, u32[]{:S(2)}) collective-permute-start(bf16[1,8,1,256]{3,2,1,0:T(2,128)(2,1)S(1)} %get-tuple-element.41), channel_id=1, source_target_pairs={{0,1},{1,2},{2,3},{3,4},{4,5},{5,6},{6,7},{7,8},{8,9},{9,10},{10,1... | collective-permute-start | bytes 12296 | tf_op jit(solution)/shard_map/ppermute | solution.py:12
  22.4 8.1 %collective-permute-start.3 = (bf16[1,1,82,256]{3,2,1,0:T(8,128)(2,1)S(1)}, bf16[1,1,82,256]{3,2,1,0:T(8,128)(2,1)S(1)}, u32[]{:S(2)}, u32[]{:S(2)}) collective-permute-start(bf16[1,1,82,256]{3,2,1,0:T(8,128)(2,1)S(1)} %get-tuple-element.30), channel_id=1, source_target_pairs={{8,0},{9,1},{10,2},{11,3},{12,4},{13,5},{14,6},{15,7},{16,8},{17,9... | collective-permute-start | bytes 125960 | tf_op jit(solution)/shard_map/ppermute | solution.py:12
  24.3 8.3 %collective-permute-start.2 = (bf16[1,1,82,256]{3,2,1,0:T(8,128)(2,1)S(1)}, bf16[1,1,82,256]{3,2,1,0:T(8,128)(2,1)S(1)}, u32[]{:S(2)}, u32[]{:S(2)}) collective-permute-start(bf16[1,1,82,256]{3,2,1,0:T(8,128)(2,1)S(1)} %get-tuple-element.29), channel_id=1, source_target_pairs={{0,8},{1,9},{2,10},{3,11},{4,12},{5,13},{6,14},{7,15},{8,16},{9,17... | collective-permute-start | bytes 125960 | tf_op jit(solution)/shard_map/ppermute | solution.py:12
  35.5 6.6 %collective-permute-start.4 = (bf16[8,80,128]{2,1,0:T(8,128)(2,1)S(1)}, bf16[8,80,128]{2,1,0:T(8,128)(2,1)S(1)}, u32[]{:S(2)}, u32[]{:S(2)}) collective-permute-start(bf16[8,80,128]{2,1,0:T(8,128)(2,1)S(1)} %bitcast.69), channel_id=1, source_target_pairs={{0,64},{64,128},{128,192},{1,65},{65,129},{129,193},{2,66},{66,130... | collective-permute-start | bytes 491528 | tf_op jit(solution)/shard_map/ppermute | solution.py:12
  42.2 6.8 %collective-permute-start.6 = (bf16[1,8,1,256]{3,2,1,0:T(2,128)(2,1)S(1)}, bf16[1,8,1,256]{3,2,1,0:T(2,128)(2,1)S(1)}, u32[]{:S(2)}, u32[]{:S(2)}) collective-permute-start(bf16[1,8,1,256]{3,2,1,0:T(2,128)(2,1)S(1)} %get-tuple-element.40), channel_id=1, source_target_pairs={{1,0},{2,1},{3,2},{4,3},{5,4},{6,5},{7,6},{8,7},{9,8},{10,9},{11,1... | collective-permute-start | bytes 12296 | tf_op jit(solution)/shard_map/ppermute | solution.py:12
  44.2 10.7 %collective-permute-start.5 = (bf16[1,8,1,256]{3,2,1,0:T(2,128)(2,1)S(1)}, bf16[1,8,1,256]{3,2,1,0:T(2,128)(2,1)S(1)}, u32[]{:S(2)}, u32[]{:S(2)}) collective-permute-start(bf16[1,8,1,256]{3,2,1,0:T(2,128)(2,1)S(1)} %get-tuple-element.39), channel_id=1, source_target_pairs={{0,1},{1,2},{2,3},{3,4},{4,5},{5,6},{6,7},{7,8},{8,9},{9,10},{10,1... | collective-permute-start | bytes 12296 | tf_op jit(solution)/shard_map/ppermute | solution.py:12
  54.9 7.4 %collective-permute-start.8 = (bf16[1,1,82,256]{3,2,1,0:T(8,128)(2,1)S(1)}, bf16[1,1,82,256]{3,2,1,0:T(8,128)(2,1)S(1)}, u32[]{:S(2)}, u32[]{:S(2)}) collective-permute-start(bf16[1,1,82,256]{3,2,1,0:T(8,128)(2,1)S(1)} %get-tuple-element.28), channel_id=1, source_target_pairs={{8,0},{9,1},{10,2},{11,3},{12,4},{13,5},{14,6},{15,7},{16,8},{17,9... | collective-permute-start | bytes 125960 | tf_op jit(solution)/shard_map/ppermute | solution.py:12
  57.2 8.3 %collective-permute-start.7 = (bf16[1,1,82,256]{3,2,1,0:T(8,128)(2,1)S(1)}, bf16[1,1,82,256]{3,2,1,0:T(8,128)(2,1)S(1)}, u32[]{:S(2)}, u32[]{:S(2)}) collective-permute-start(bf16[1,1,82,256]{3,2,1,0:T(8,128)(2,1)S(1)} %get-tuple-element.27), channel_id=1, source_target_pairs={{0,8},{1,9},{2,10},{3,11},{4,12},{5,13},{6,14},{7,15},{8,16},{9,17... | collective-permute-start | bytes 125960 | tf_op jit(solution)/shard_map/ppermute | solution.py:12
  69.1 6.6 %collective-permute-start.9 = (bf16[8,80,128]{2,1,0:T(8,128)(2,1)S(1)}, bf16[8,80,128]{2,1,0:T(8,128)(2,1)S(1)}, u32[]{:S(2)}, u32[]{:S(2)}) collective-permute-start(bf16[8,80,128]{2,1,0:T(8,128)(2,1)S(1)} %broadcast_select_fusion.7), channel_id=1, source_target_pairs={{0,64},{64,128},{128,192},{1,65},{65,129},{129,193},{2,66},{66,130... | collective-permute-start | bytes 491528 | tf_op jit(solution)/shard_map/ppermute | solution.py:12
  75.8 6.8 %collective-permute-start.11 = (bf16[1,8,1,256]{3,2,1,0:T(2,128)(2,1)S(1)}, bf16[1,8,1,256]{3,2,1,0:T(2,128)(2,1)S(1)}, u32[]{:S(2)}, u32[]{:S(2)}) collective-permute-start(bf16[1,8,1,256]{3,2,1,0:T(2,128)(2,1)S(1)} %get-tuple-element.38), channel_id=1, source_target_pairs={{1,0},{2,1},{3,2},{4,3},{5,4},{6,5},{7,6},{8,7},{9,8},{10,9},{11,1... | collective-permute-start | bytes 12296 | tf_op jit(solution)/shard_map/ppermute | solution.py:12
  77.8 10.7 %collective-permute-start.10 = (bf16[1,8,1,256]{3,2,1,0:T(2,128)(2,1)S(1)}, bf16[1,8,1,256]{3,2,1,0:T(2,128)(2,1)S(1)}, u32[]{:S(2)}, u32[]{:S(2)}) collective-permute-start(bf16[1,8,1,256]{3,2,1,0:T(2,128)(2,1)S(1)} %get-tuple-element.37), channel_id=1, source_target_pairs={{0,1},{1,2},{2,3},{3,4},{4,5},{5,6},{6,7},{7,8},{8,9},{9,10},{10,1... | collective-permute-start | bytes 12296 | tf_op jit(solution)/shard_map/ppermute | solution.py:12
  89.1 8.0 %collective-permute-start.13 = (bf16[1,1,82,256]{3,2,1,0:T(8,128)(2,1)}, bf16[1,1,82,256]{3,2,1,0:T(8,128)(2,1)}, u32[]{:S(2)}, u32[]{:S(2)}) collective-permute-start(bf16[1,1,82,256]{3,2,1,0:T(8,128)(2,1)} %get-tuple-element.26), channel_id=1, source_target_pairs={{8,0},{9,1},{10,2},{11,3},{12,4},{13,5},{14,6},{15,7},{16,8},{17,9... | collective-permute-start | bytes 125960 | tf_op jit(solution)/shard_map/ppermute | solution.py:12
  91.0 8.7 %collective-permute-start.12 = (bf16[1,1,82,256]{3,2,1,0:T(8,128)(2,1)}, bf16[1,1,82,256]{3,2,1,0:T(8,128)(2,1)}, u32[]{:S(2)}, u32[]{:S(2)}) collective-permute-start(bf16[1,1,82,256]{3,2,1,0:T(8,128)(2,1)} %get-tuple-element.25), channel_id=1, source_target_pairs={{0,8},{1,9},{2,10},{3,11},{4,12},{5,13},{6,14},{7,15},{8,16},{9,17... | collective-permute-start | bytes 125960 | tf_op jit(solution)/shard_map/ppermute | solution.py:12
  104.1 6.6 %collective-permute-start.14 = (bf16[8,80,128]{2,1,0:T(8,128)(2,1)S(1)}, bf16[8,80,128]{2,1,0:T(8,128)(2,1)S(1)}, u32[]{:S(2)}, u32[]{:S(2)}) collective-permute-start(bf16[8,80,128]{2,1,0:T(8,128)(2,1)S(1)} %broadcast_select_fusion.6), channel_id=1, source_target_pairs={{0,64},{64,128},{128,192},{1,65},{65,129},{129,193},{2,66},{66,130... | collective-permute-start | bytes 491528 | tf_op jit(solution)/shard_map/ppermute | solution.py:12
  110.8 6.8 %collective-permute-start.16 = (bf16[1,8,1,256]{3,2,1,0:T(2,128)(2,1)S(1)}, bf16[1,8,1,256]{3,2,1,0:T(2,128)(2,1)S(1)}, u32[]{:S(2)}, u32[]{:S(2)}) collective-permute-start(bf16[1,8,1,256]{3,2,1,0:T(2,128)(2,1)S(1)} %get-tuple-element.36), channel_id=1, source_target_pairs={{1,0},{2,1},{3,2},{4,3},{5,4},{6,5},{7,6},{8,7},{9,8},{10,9},{11,1... | collective-permute-start | bytes 12296 | tf_op jit(solution)/shard_map/ppermute | solution.py:12
  112.8 10.7 %collective-permute-start.15 = (bf16[1,8,1,256]{3,2,1,0:T(2,128)(2,1)S(1)}, bf16[1,8,1,256]{3,2,1,0:T(2,128)(2,1)S(1)}, u32[]{:S(2)}, u32[]{:S(2)}) collective-permute-start(bf16[1,8,1,256]{3,2,1,0:T(2,128)(2,1)S(1)} %get-tuple-element.35), channel_id=1, source_target_pairs={{0,1},{1,2},{2,3},{3,4},{4,5},{5,6},{6,7},{7,8},{8,9},{9,10},{10,1... | collective-permute-start | bytes 12296 | tf_op jit(solution)/shard_map/ppermute | solution.py:12
  123.5 7.4 %collective-permute-start.18 = (bf16[1,1,82,256]{3,2,1,0:T(8,128)(2,1)S(1)}, bf16[1,1,82,256]{3,2,1,0:T(8,128)(2,1)S(1)}, u32[]{:S(2)}, u32[]{:S(2)}) collective-permute-start(bf16[1,1,82,256]{3,2,1,0:T(8,128)(2,1)S(1)} %get-tuple-element.24), channel_id=1, source_target_pairs={{8,0},{9,1},{10,2},{11,3},{12,4},{13,5},{14,6},{15,7},{16,8},{17,9... | collective-permute-start | bytes 125960 | tf_op jit(solution)/shard_map/ppermute | solution.py:12
  125.9 8.3 %collective-permute-start.17 = (bf16[1,1,82,256]{3,2,1,0:T(8,128)(2,1)S(1)}, bf16[1,1,82,256]{3,2,1,0:T(8,128)(2,1)S(1)}, u32[]{:S(2)}, u32[]{:S(2)}) collective-permute-start(bf16[1,1,82,256]{3,2,1,0:T(8,128)(2,1)S(1)} %get-tuple-element.23), channel_id=1, source_target_pairs={{0,8},{1,9},{2,10},{3,11},{4,12},{5,13},{6,14},{7,15},{8,16},{9,17... | collective-permute-start | bytes 125960 | tf_op jit(solution)/shard_map/ppermute | solution.py:12
  137.8 8.7 %copy-start.9 = (bf16[640,128]{1,0:T(8,128)(2,1)}, bf16[640,128]{1,0:T(8,128)(2,1)S(1)}, u32[]{:S(2)}) copy-start(bf16[640,128]{1,0:T(8,128)(2,1)S(1)} %get-tuple-element.7) | copy-start | bytes 491524
  137.8 6.6 %collective-permute-start.19 = (bf16[8,80,128]{2,1,0:T(8,128)(2,1)S(1)}, bf16[8,80,128]{2,1,0:T(8,128)(2,1)S(1)}, u32[]{:S(2)}, u32[]{:S(2)}) collective-permute-start(bf16[8,80,128]{2,1,0:T(8,128)(2,1)S(1)} %broadcast_select_fusion.4), channel_id=1, source_target_pairs={{0,64},{64,128},{128,192},{1,65},{65,129},{129,193},{2,66},{66,130... | collective-permute-start | bytes 491528 | tf_op jit(solution)/shard_map/ppermute | solution.py:12
  144.5 6.9 %collective-permute-start.21 = (bf16[1,8,1,256]{3,2,1,0:T(2,128)(2,1)S(1)}, bf16[1,8,1,256]{3,2,1,0:T(2,128)(2,1)S(1)}, u32[]{:S(2)}, u32[]{:S(2)}) collective-permute-start(bf16[1,8,1,256]{3,2,1,0:T(2,128)(2,1)S(1)} %get-tuple-element.34), channel_id=1, source_target_pairs={{1,0},{2,1},{3,2},{4,3},{5,4},{6,5},{7,6},{8,7},{9,8},{10,9},{11,1... | collective-permute-start | bytes 12296 | tf_op jit(solution)/shard_map/ppermute | solution.py:12
  146.6 10.7 %collective-permute-start.20 = (bf16[1,8,1,256]{3,2,1,0:T(2,128)(2,1)S(1)}, bf16[1,8,1,256]{3,2,1,0:T(2,128)(2,1)S(1)}, u32[]{:S(2)}, u32[]{:S(2)}) collective-permute-start(bf16[1,8,1,256]{3,2,1,0:T(2,128)(2,1)S(1)} %get-tuple-element.33), channel_id=1, source_target_pairs={{0,1},{1,2},{2,3},{3,4},{4,5},{5,6},{6,7},{7,8},{8,9},{9,10},{10,1... | collective-permute-start | bytes 12296 | tf_op jit(solution)/shard_map/ppermute | solution.py:12
  157.3 7.6 %collective-permute-start.23 = (bf16[1,1,82,256]{3,2,1,0:T(8,128)(2,1)S(1)}, bf16[1,1,82,256]{3,2,1,0:T(8,128)(2,1)S(1)}, u32[]{:S(2)}, u32[]{:S(2)}) collective-permute-start(bf16[1,1,82,256]{3,2,1,0:T(8,128)(2,1)S(1)} %get-tuple-element.22), channel_id=1, source_target_pairs={{8,0},{9,1},{10,2},{11,3},{12,4},{13,5},{14,6},{15,7},{16,8},{17,9... | collective-permute-start | bytes 125960 | tf_op jit(solution)/shard_map/ppermute | solution.py:12
  159.3 8.3 %collective-permute-start.22 = (bf16[1,1,82,256]{3,2,1,0:T(8,128)(2,1)S(1)}, bf16[1,1,82,256]{3,2,1,0:T(8,128)(2,1)S(1)}, u32[]{:S(2)}, u32[]{:S(2)}) collective-permute-start(bf16[1,1,82,256]{3,2,1,0:T(8,128)(2,1)S(1)} %get-tuple-element.21), channel_id=1, source_target_pairs={{0,8},{1,9},{2,10},{3,11},{4,12},{5,13},{6,14},{7,15},{8,16},{9,17... | collective-permute-start | bytes 125960 | tf_op jit(solution)/shard_map/ppermute | solution.py:12
  170.1 9.6 %copy-start.10 = (bf16[640,128]{1,0:T(8,128)(2,1)S(1)}, bf16[640,128]{1,0:T(8,128)(2,1)}, u32[]{:S(2)}) copy-start(bf16[640,128]{1,0:T(8,128)(2,1)} %copy-done.9) | copy-start | bytes 491524
  171.0 6.6 %collective-permute-start.24 = (bf16[8,80,128]{2,1,0:T(8,128)(2,1)S(1)}, bf16[8,80,128]{2,1,0:T(8,128)(2,1)S(1)}, u32[]{:S(2)}, u32[]{:S(2)}) collective-permute-start(bf16[8,80,128]{2,1,0:T(8,128)(2,1)S(1)} %broadcast_select_fusion.2), channel_id=1, source_target_pairs={{0,64},{64,128},{128,192},{1,65},{65,129},{129,193},{2,66},{66,130... | collective-permute-start | bytes 491528 | tf_op jit(solution)/shard_map/ppermute | solution.py:12
  177.7 6.8 %collective-permute-start.26 = (bf16[1,8,1,256]{3,2,1,0:T(2,128)(2,1)S(1)}, bf16[1,8,1,256]{3,2,1,0:T(2,128)(2,1)S(1)}, u32[]{:S(2)}, u32[]{:S(2)}) collective-permute-start(bf16[1,8,1,256]{3,2,1,0:T(2,128)(2,1)S(1)} %get-tuple-element.32), channel_id=1, source_target_pairs={{1,0},{2,1},{3,2},{4,3},{5,4},{6,5},{7,6},{8,7},{9,8},{10,9},{11,1... | collective-permute-start | bytes 12296 | tf_op jit(solution)/shard_map/ppermute | solution.py:12
  179.8 10.7 %collective-permute-start.25 = (bf16[1,8,1,256]{3,2,1,0:T(2,128)(2,1)S(1)}, bf16[1,8,1,256]{3,2,1,0:T(2,128)(2,1)S(1)}, u32[]{:S(2)}, u32[]{:S(2)}) collective-permute-start(bf16[1,8,1,256]{3,2,1,0:T(2,128)(2,1)S(1)} %get-tuple-element.31), channel_id=1, source_target_pairs={{0,1},{1,2},{2,3},{3,4},{4,5},{5,6},{6,7},{7,8},{8,9},{9,10},{10,1... | collective-permute-start | bytes 12296 | tf_op jit(solution)/shard_map/ppermute | solution.py:12
  190.5 7.4 %collective-permute-start.28 = (bf16[1,1,82,256]{3,2,1,0:T(8,128)(2,1)S(1)}, bf16[1,1,82,256]{3,2,1,0:T(8,128)(2,1)S(1)}, u32[]{:S(2)}, u32[]{:S(2)}) collective-permute-start(bf16[1,1,82,256]{3,2,1,0:T(8,128)(2,1)S(1)} %get-tuple-element.20), channel_id=1, source_target_pairs={{8,0},{9,1},{10,2},{11,3},{12,4},{13,5},{14,6},{15,7},{16,8},{17,9... | collective-permute-start | bytes 125960 | tf_op jit(solution)/shard_map/ppermute | solution.py:12
  192.4 8.3 %collective-permute-start.27 = (bf16[1,1,82,256]{3,2,1,0:T(8,128)(2,1)S(1)}, bf16[1,1,82,256]{3,2,1,0:T(8,128)(2,1)S(1)}, u32[]{:S(2)}, u32[]{:S(2)}) collective-permute-start(bf16[1,1,82,256]{3,2,1,0:T(8,128)(2,1)S(1)} %get-tuple-element.19), channel_id=1, source_target_pairs={{0,8},{1,9},{2,10},{3,11},{4,12},{5,13},{6,14},{7,15},{8,16},{9,17... | collective-permute-start | bytes 125960 | tf_op jit(solution)/shard_map/ppermute | solution.py:12
  (10 other events, 34.4 us)
where the time goes:
time: 206 us; the launch traced here: 205 us
  starting transfers between devices  99.8 us (48%)
  waiting for transfers between devices  78.2 us (38%)
  matrix products  10.1 us (5%)
  other arithmetic  9.51 us (5%)
  local copies, waits for them, and re-layouts  5.99 us (3%)
    ppermute x29, starting transfers between devices, shifted(): lax.ppermute(value, axis, [(source, source + steps) for source in range(f...  99.8 us
    ppermute x29, waiting for transfers between devices, shifted(): lax.ppermute(value, axis, [(source, source + steps) for source in range(f...  78.2 us
    dot_general x6, matrix products, advance(): jnp.dot(columns, kernel, preferred_element_type=jnp.float32) + gate_bias  10.1 us
  transfers between devices with their start and end apart: 29, of which 19 were waited for; matrix products, arithmetic and copies ran while one was open for 1% of the time, Pallas kernels for 0%

commit v1 on v0

v1 whole, which is shorter than its diff:
```python
import functools

import jax
import jax.numpy as jnp
from jax import lax
from jax.experimental import pallas as pl
from jax.experimental.pallas import tpu as pltpu
from jax.sharding import PartitionSpec as P

MESH = pl.DeviceIdType.MESH
TCOLS = 8
TROWS = 8
C = 128
CX, CY, TIME = 80, 8, 3
HALF = CX // 2
TOP = 4
ROWS = CY + 2 * TOP
WIDE = 48
FIRST = 64
FW = 80
IW = 88
CHUNKS = {14: (4, 3, 3, 4), 12: (4, 4, 4), 10: (5, 5), 8: (4, 4)}
BF, F32 = jnp.bfloat16, jnp.float32


def sigmoid(v):
    return 0.5 * jnp.tanh(0.5 * v) + 0.5


def kernel(
    frames, weights, bias, out_h, out_c,
    fr, s32, fyb, hb, hz, fin, zin0, zin, zh, f0, f1, cell, wv, bv, hs, cs,
    local_sem, w_send, w_recv, fr_send, fr_recv, z_send, z_recv, o_send, o_recv,
):
    section, tile = lax.axis_index("section"), lax.axis_index("tile")
    stage, core = section // 2, section % 2
    first_stage = stage == 0
    row, col = tile // TCOLS, tile % TCOLS
    has_n, has_s = row > 0, row < TROWS - 1
    has_side = jnp.where(core == 0, col > 0, col < TCOLS - 1)
    side = 2 * core - 1
    partner = (2 * stage + 1 - core, tile)

    def at(stage_of, core_of, tile_of):
        return (2 * stage_of + core_of, tile_of)

    own_w = [
        pltpu.make_async_copy(
            weights.at[0, :, :, pl.ds(C * p, C), :], wv.at[core, :, :, pl.ds(C * p, C), :], local_sem.at[p]
        )
        for p in range(2)
    ]
    load_f = pltpu.make_async_copy(frames.at[:, 0], fr, local_sem.at[2])

    @pl.when(first_stage)
    def _():
        load_f.start()

    for cp in own_w:
        cp.start()

    def bias_copy():
        return pltpu.make_async_remote_copy(
            src_ref=bv.at[core], dst_ref=bv.at[core], send_sem=w_send.at[2], recv_sem=w_recv.at[2],
            device_id=partner, device_id_type=MESH,
        )

    def weight_copy(p):
        return pltpu.make_async_remote_copy(
            src_ref=weights.at[0, :, :, pl.ds(C * p, C), :], dst_ref=wv.at[core, :, :, pl.ds(C * p, C), :],
            send_sem=w_send.at[p], recv_sem=w_recv.at[p], device_id=partner, device_id_type=MESH,
        )

    cols48 = pl.multiple_of(32 * core, 16)
    to48 = pl.multiple_of(16 * (1 - core), 16)
    cols16 = pl.multiple_of(64 * core, 16)
    to16 = pl.multiple_of(48 * (1 - core), 16)

    def frame_copies(t):
        n = TOP - t

        def copy(kind, from_row, to_row, count, wide, target):
            src = fyb.at[t, pl.ds(from_row, count), pl.ds(cols48, WIDE) if wide else pl.ds(cols16, 16)]
            dst = hb.at[t, pl.ds(to_row, count), pl.ds(to48, WIDE) if wide else pl.ds(to16, 16)]
            return pltpu.make_async_remote_copy(
                src_ref=src, dst_ref=dst, send_sem=fr_send.at[t, kind], recv_sem=fr_recv.at[t, kind],
                device_id=target, device_id_type=MESH,
            )

        return [
            (has_s, has_n, copy(0, CY - n, TOP - n, n, True, at(0, core, tile + TCOLS))),
            (has_n, has_s, copy(1, 0, TOP + CY, n, True, at(0, core, tile - TCOLS))),
            (has_side, has_side, copy(2, 0, TOP, CY, False, at(0, 1 - core, tile + side))),
            (has_side & has_s, has_side & has_n, copy(3, CY - n, TOP - n, n, False, at(0, 1 - core, tile + side + TCOLS))),
            (has_side & has_n, has_side & has_s, copy(4, 0, TOP + CY, n, False, at(0, 1 - core, tile + side - TCOLS))),
        ]

    def own_frame(t):
        return pltpu.make_async_copy(
            fyb.at[t, :, pl.ds(cols48, WIDE)], hb.at[t, pl.ds(TOP, CY), pl.ds(to48, WIDE)], local_sem.at[4 + t]
        )

    def stage_copies(t):
        k = TIME - 1 - t

        def copy(kind, from_row, to_row, count, target):
            return pltpu.make_async_remote_copy(
                src_ref=zh.at[1, t, 1, pl.ds((TOP + from_row) * WIDE, count * WIDE)],
                dst_ref=hz.at[t, pl.ds((TOP + to_row) * WIDE, count * WIDE)],
                send_sem=z_send.at[t, kind], recv_sem=z_recv.at[t, kind], device_id=target, device_id_type=MESH,
            )

        return [
            (has_s, has_n, copy(0, CY - 2 - k, -2 - k, 2, at(1, core, tile + TCOLS))),
            (has_n, has_s, copy(1, k, CY + k, 2, at(1, core, tile - TCOLS))),
            (None, None, copy(2, -k, -k, CY + 2 * k, at(1, core, tile))),
        ]

    def when(condition, action):
        if condition is None:
            action()
        else:
            pl.when(condition)(action)

    bv[core] = jnp.broadcast_to(bias[...].astype(F32), (8, 4 * C))
    f0[...] = jnp.zeros_like(f0)
    f1[...] = jnp.zeros_like(f1)
    fin[...] = jnp.zeros_like(fin)

    @pl.when(first_stage)
    def _():
        hb[...] = jnp.zeros_like(hb)
        load_f.wait()
        for t in range(TIME):
            for x in range(CX):
                s32[CY * x : CY * (x + 1), :] = fr[t, :, C * x : C * (x + 1)].astype(F32)
            for y in range(CY):
                fyb[t, y] = s32[pl.ds(y, CX, stride=CY), :].astype(BF)
            own_frame(t).start()

    @pl.when(jnp.logical_not(first_stage))
    def _():
        hz[...] = jnp.zeros_like(hz)

    barrier = pltpu.get_barrier_semaphore()

    def greet(device):
        pl.semaphore_signal(barrier, inc=1, device_id=device, device_id_type=MESH)

    def met():
        pl.semaphore_wait(barrier, 1)

    greet(partner)
    greet(at(1 - stage, core, tile))
    pl.when(has_n)(lambda: greet(at(1 - stage, core, tile - TCOLS)))
    pl.when(has_s)(lambda: greet(at(1 - stage, core, tile + TCOLS)))

    @pl.when(first_stage)
    def _():
        pl.when(has_n)(lambda: greet(at(0, core, tile - TCOLS)))
        pl.when(has_s)(lambda: greet(at(0, core, tile + TCOLS)))
        pl.when(has_side)(lambda: greet(at(0, 1 - core, tile + side)))
        pl.when(has_side & has_n)(lambda: greet(at(0, 1 - core, tile + side - TCOLS)))
        pl.when(has_side & has_s)(lambda: greet(at(0, 1 - core, tile + side + TCOLS)))

    one = lambda c: c.astype(jnp.int32)
    near = one(has_n) + one(has_s)
    mine = 2 + near
    tiles = near + one(has_side) + one(has_side & has_n) + one(has_side & has_s)
    pl.semaphore_wait(barrier, mine + jnp.where(first_stage, tiles, 0))

    bias_copy().start()

    @pl.when(first_stage)
    def _():
        for sends, _, cp in frame_copies(0):
            pl.when(sends)(cp.start)

    weight_copy(0).start()

    @pl.when(first_stage)
    def _():
        for t in range(1, TIME):
            for sends, _, cp in frame_copies(t):
                pl.when(sends)(cp.start)

    weight_copy(1).start()

    def column_mask(width, first):
        x = lax.broadcasted_iota(jnp.int32, (width, C), 0) + (first + HALF * core + CX * col)
        return (x >= 0) & (x < CX * TCOLS)

    masks = {WIDE: column_mask(WIDE, -4), FIRST: column_mask(FIRST, -12)}

    def put_input(t, first_column):
        width = FIRST if t == 0 else WIDE
        target = zin0 if t == 0 else zin.at[t - 1]
        for y in range(t, ROWS - t):
            for b in range(3):
                begin = y * IW + first_column + b - 1
                target[b, y * width : (y + 1) * width, :] = fin[begin : begin + width, :].astype(BF)

    def get_input(t):
        @pl.when(first_stage)
        def _():
            own_frame(t).wait()
            for _, gets, cp in frame_copies(t):
                pl.when(gets)(cp.wait_recv)
            for y in range(t, ROWS - t):
                fin[pl.ds(pl.multiple_of(y * IW + 8 + 8 * core, 8), FIRST), :] = hb[t, y].astype(F32)
            put_input(t, 12 if t == 0 else 20)

        @pl.when(jnp.logical_not(first_stage))
        def _():
            for _, gets, cp in stage_copies(t):
                when(gets, cp.wait_recv)
            for y in range(t, ROWS - t):
                fin[y * IW + 24 : y * IW + 24 + WIDE, :] = hz[t, y * WIDE : (y + 1) * WIDE, :].astype(F32)
            put_input(t, 16 if t == 0 else 24)

    def step(layer, t):
        k = (1 - layer) + (TIME - 1 - t)
        width = FIRST if (layer == 0 and t == 0) else WIDE
        hidden = f0 if layer == 0 else f1
        if layer == 1:
            source = zh.at[0, t]
        else:
            source = zin0 if t == 0 else zin.at[t - 1]
        if t == 0:
            kernel_of = wv[layer, :, :, :C, :].reshape(9 * C, 4 * C)
        else:
            kernel_of = wv[layer].reshape(18 * C, 4 * C)
        gate_bias = bv[layer, 0:1, :]
        y = -k
        for count in CHUNKS[CY + 2 * k]:
            pieces = []
            for a in range(3):
                rows = pl.ds((y + a - 1 + TOP) * width, count * width)
                for b in range(3):
                    pieces.append(source[b, rows, :])
                    if t > 0:
                        pieces.append(zh[layer, t - 1, b, rows, :])
            gates = jnp.dot(jnp.concatenate(pieces, axis=1), kernel_of, preferred_element_type=F32) + gate_bias
            c_new = sigmoid(gates[:, :C]) * jnp.tanh(gates[:, 3 * C :])
            cells = pl.ds((y + TOP) * WIDE, count * WIDE)
            if t > 0:
                c_new = sigmoid(gates[:, C : 2 * C]) * cell[layer, cells, :] + c_new
            h_new = sigmoid(gates[:, 2 * C : 3 * C]) * jnp.tanh(c_new)
            for i in range(count):
                line = y + i
                inside = masks[width]
                if line < 0:
                    inside = inside & has_n
                if line >= CY:
                    inside = inside & has_s
                h_row = jnp.where(inside, h_new[i * width : (i + 1) * width, :], 0.0)
                begin = (line + TOP) * FW + 16
                edge = (width - WIDE) // 2
                hidden[begin - edge : begin + WIDE + edge, :] = h_row
                cell[layer, (line + TOP) * WIDE : (line + TOP + 1) * WIDE, :] = c_new[i * width + edge : (i + 1) * width - edge, :]
                for b in range(3):
                    zh[layer, t, b, (line + TOP) * WIDE : (line + TOP + 1) * WIDE, :] = hidden[
                        begin + b - 1 : begin + b - 1 + WIDE, :
                    ].astype(BF)
            y += count

    def result_copies(layer, src, dst, slot):
        local = pltpu.make_async_copy(src, dst, local_sem.at[8 + slot])
        remote = pltpu.make_async_remote_copy(
            src_ref=src, dst_ref=dst, send_sem=o_send.at[slot], recv_sem=o_recv.at[slot],
            device_id=partner, device_id_type=MESH,
        )
        return core == layer, local, remote

    half = pl.ds(pl.multiple_of(core * (HALF * C), C), HALF * C)

    def hidden_copies(layer, t):
        return result_copies(layer, hs.at[layer, t], out_h.at[0, t, 0, :, half], t)

    def cell_copies(layer):
        return result_copies(layer, cs.at[layer], out_c.at[0, 0, :, half], TIME)

    def send(copies):
        here, local, remote = copies
        pl.when(here)(local.start)
        pl.when(jnp.logical_not(here))(remote.start)

    def finish(copies):
        here, local, remote = copies

        @pl.when(here)
        def _():
            local.wait()
            remote.wait_recv()

        pl.when(jnp.logical_not(here))(remote.wait_send)

    def put_hidden(layer, t):
        hidden = f0 if layer == 0 else f1
        for x in range(HALF):
            hs[layer, t, :, C * x : C * (x + 1)] = hidden[pl.ds(TOP * FW + 20 + x, CY, stride=FW), :].astype(BF)
        send(hidden_copies(layer, t))

    def put_cell(layer):
        for x in range(HALF):
            cs[layer, :, C * x : C * (x + 1)] = cell[layer, pl.ds(TOP * WIDE + 4 + x, CY, stride=WIDE), :]
        send(cell_copies(layer))

    for p in range(2):
        own_w[p].wait()
    for t in range(TIME):
        get_input(t)
        if t == 0:
            bias_copy().wait_recv()
            weight_copy(0).wait_recv()
        if t == 1:
            weight_copy(1).wait_recv()
        step(0, t)
        step(1, t)

        @pl.when(first_stage)
        def _(t=t):
            for sends, _, cp in stage_copies(t):
                when(sends, cp.start)

        put_hidden(0, t)
        put_hidden(1, t)
    put_cell(0)
    put_cell(1)

    bias_copy().wait_send()
    for p in range(2):
        weight_copy(p).wait_send()

    @pl.when(first_stage)
    def _():
        for t in range(TIME):
            for sends, _, cp in frame_copies(t) + stage_copies(t):
                when(sends, cp.wait_send)

    for layer in range(2):
        for t in range(TIME):
            finish(hidden_copies(layer, t))
        finish(cell_copies(layer))


def local(frames, weights, bias):
    any_space = pl.BlockSpec(memory_space=pl.ANY)
    dma = pltpu.SemaphoreType.DMA
    return pl.pallas_call(
        kernel,
        out_shape=(
            jax.ShapeDtypeStruct((1, TIME, 1, CY, CX * C), BF),
            jax.ShapeDtypeStruct((1, 1, CY, CX * C), F32),
        ),
        in_specs=[any_space, any_space, pl.BlockSpec(memory_space=pltpu.VMEM)],
        out_specs=(any_space, any_space),
        scratch_shapes=[
            pltpu.VMEM((TIME, CY, CX * C), BF),
            pltpu.VMEM((CY * CX, C), F32),
            pltpu.VMEM((TIME, CY, CX, C), BF),
            pltpu.VMEM((TIME, ROWS, FIRST, C), BF),
            pltpu.VMEM((TIME, ROWS * WIDE, C), BF),
            pltpu.VMEM((ROWS * IW, C), F32),
            pltpu.VMEM((3, ROWS * FIRST, C), BF),
            pltpu.VMEM((TIME - 1, 3, ROWS * WIDE, C), BF),
            pltpu.VMEM((2, TIME, 3, ROWS * WIDE, C), BF),
            pltpu.VMEM((ROWS * FW, C), F32),
            pltpu.VMEM((ROWS * FW, C), F32),
            pltpu.VMEM((2, ROWS * WIDE, C), F32),
            pltpu.VMEM((2, 3, 3, 2 * C, 4 * C), BF),
            pltpu.VMEM((2, 8, 4 * C), F32),
            pltpu.VMEM((2, TIME, CY, HALF * C), BF),
            pltpu.VMEM((2, CY, HALF * C), F32),
            dma((12,)),
            dma((3,)),
            dma((3,)),
            dma((TIME, 5)),
            dma((TIME, 5)),
            dma((TIME, 3)),
            dma((TIME, 3)),
            dma((TIME + 1,)),
            dma((TIME + 1,)),
        ],
        compiler_params=pltpu.CompilerParams(
            collective_id=0, has_side_effects=True, vmem_limit_bytes=48 * 2**20
        ),
    )(frames, weights, bias)


def solution(mesh):
    return jax.shard_map(
        local,
        mesh=mesh,
        in_specs=(P(None, "tile", None, None), P("section", None, None, None, None), P("section", None)),
        out_specs=(P("section", None, "tile", None, None), P("section", "tile", None, None)),
        check_vma=False,
    )
```

time: 206 us -> 39.7 us (0.19)
  the two profiles are of different devices: /device:TPU:56 before, /device:TPU:43 now
where the time goes in v1:
time: 39.7 us; the launch traced here: 39.5 us
  Pallas kernels  34 us (86%)
  local copies, waits for them, and re-layouts  4.87 us (12%)
  between operations  0.65 us (2%)
    pallas_call x1, Pallas kernels, local(): pl.pallas_call(kernel, out_shape=(jax.ShapeDtypeStruct((1, TIME, 1, CY, C...  34 us
    unnamed x8, local copies, waits for them, and re-layouts  4.87 us

profile of v1, /device:TPU:43, one launch (start us, length us, event | category | flops | bytes accessed | tf_op | source)
XLA Modules:
  0.0 39.5 jit_solution(2031275965052744716)
XLA Ops:
  0.6 0.0 copy-start
  0.6 1.7 %copy-done = bf16[1,3,3,256,512]{4,3,2,1,0:T(8,128)(2,1)S(1)} copy-done((bf16[1,3,3,256,512]{4,3,2,1,0:T(8,128)(2,1)S(1)}, bf16[1,3,3,256,512]{4,3,2,1,0:T(8,128)(2,1)}, u32[]{:S(2)}) %copy-start) | copy-done | bytes 2359320
  2.3 0.0 copy-start.1
  2.3 1.0 %copy-done.1 = bf16[3,1,8,10240]{3,2,1,0:T(8,128)(2,1)S(1)} copy-done((bf16[3,1,8,10240]{3,2,1,0:T(8,128)(2,1)S(1)}, bf16[3,1,8,10240]{3,2,1,0:T(8,128)(2,1)}, u32[]{:S(2)}) %copy-start.1) | copy-done | bytes 491544
  3.3 0.0 copy-start.2
  3.3 0.7 %copy-done.2 = bf16[1,512]{1,0:T(2,128)(2,1)S(1)} copy-done((bf16[1,512]{1,0:T(2,128)(2,1)S(1)}, bf16[1,512]{1,0:T(2,128)(2,1)}, u32[]{:S(2)}) %copy-start.2) | copy-done | bytes 1048
  4.0 34.0 %shard_map.50 = (bf16[1,3,1,8,10240]{4,3,2,1,0:T(8,128)(2,1)S(1)}, f32[1,1,8,10240]{3,2,1,0:T(8,128)S(1)}) custom-call(bf16[3,1,8,10240]{3,2,1,0:T(8,128)(2,1)S(1)} %copy-done.1, bf16[1,3,3,256,512]{4,3,2,1,0:T(8,128)(2,1)S(1)} %copy-done, bf16[1,512]{1,0:T(2,128)(2,1)S(1)} %copy-done.2), custom_call_target="tpu_custom_call" | custom-call | tf_op jit(solution)/shard_map/pallas_call | solution.py:350
  38.0 0.8 %copy.7 = bf16[1,3,1,8,10240]{4,3,2,1,0:T(8,128)(2,1)} copy(bf16[1,3,1,8,10240]{4,3,2,1,0:T(8,128)(2,1)S(1)} %get-tuple-element.4) | data formatting | bytes 983040
  38.8 0.7 %copy.8 = f32[1,1,8,10240]{3,2,1,0:T(8,128)} copy(f32[1,1,8,10240]{3,2,1,0:T(8,128)S(1)} %get-tuple-element.5) | data formatting | bytes 655360
Async XLA Ops:
  0.6 1.7 %copy-start = (bf16[1,3,3,256,512]{4,3,2,1,0:T(8,128)(2,1)S(1)}, bf16[1,3,3,256,512]{4,3,2,1,0:T(8,128)(2,1)}, u32[]{:S(2)}) copy-start(bf16[1,3,3,256,512]{4,3,2,1,0:T(8,128)(2,1)} %weights.1) | copy-start | bytes 7077892
  2.3 1.0 %copy-start.1 = (bf16[3,1,8,10240]{3,2,1,0:T(8,128)(2,1)S(1)}, bf16[3,1,8,10240]{3,2,1,0:T(8,128)(2,1)}, u32[]{:S(2)}) copy-start(bf16[3,1,8,10240]{3,2,1,0:T(8,128)(2,1)} %frames.1) | copy-start | bytes 1474564
  3.3 0.7 %copy-start.2 = (bf16[1,512]{1,0:T(2,128)(2,1)S(1)}, bf16[1,512]{1,0:T(2,128)(2,1)}, u32[]{:S(2)}) copy-start(bf16[1,512]{1,0:T(2,128)(2,1)} %bias.1) | copy-start | bytes 3076

commit v2 on v1

v2 whole, which is shorter than its diff:
```python
import functools

import jax
import jax.numpy as jnp
from jax import lax
from jax.experimental import pallas as pl
from jax.experimental.pallas import tpu as pltpu
from jax.sharding import PartitionSpec as P

MESH = pl.DeviceIdType.MESH
TCOLS = 8
TROWS = 8
C = 128
CX, CY, TIME = 80, 8, 3
HALF = CX // 2
TOP = 4
ROWS = CY + 2 * TOP
WIDE = 48
FIRST = 64
FW = 80
IW = 88
CHUNKS = ({14: (4, 3, 3, 4), 12: (4, 4, 4), 10: (4, 3, 3)}, {12: (6, 6), 10: (5, 5), 8: (4, 4)})
OWN = (((-2, 4), (2, 4), (6, 4)), ((-1, 4), (3, 3), (6, 3)), ((0, 2), (6, 2), (2, 4)))
BF, F32 = jnp.bfloat16, jnp.float32


def sigmoid(v):
    return 0.5 * jnp.tanh(0.5 * v) + 0.5


def kernel(
    frames, weights, bias, out_h, out_c,
    fr, s32, fyb, hb, hz, fin, zin0, zin, zh, hid, cell, part0, part1, wv, bv, hs, cs,
    local_sem, w_send, w_recv, fr_send, fr_recv, z_send, z_recv, o_send, o_recv,
):
    section, tile = lax.axis_index("section"), lax.axis_index("tile")
    stage, core = section // 2, section % 2
    first_stage = stage == 0
    row, col = tile // TCOLS, tile % TCOLS
    has_n, has_s = row > 0, row < TROWS - 1
    has_side = jnp.where(core == 0, col > 0, col < TCOLS - 1)
    side = 2 * core - 1
    partner = (2 * stage + 1 - core, tile)

    def at(stage_of, core_of, tile_of):
        return (2 * stage_of + core_of, tile_of)

    own_w = [
        pltpu.make_async_copy(
            weights.at[0, :, :, pl.ds(C * p, C), :], wv.at[core, :, :, pl.ds(C * p, C), :], local_sem.at[p]
        )
        for p in range(2)
    ]
    load_f = pltpu.make_async_copy(frames.at[:, 0], fr, local_sem.at[2])

    @pl.when(first_stage)
    def _():
        load_f.start()

    for cp in own_w:
        cp.start()

    def bias_copy():
        return pltpu.make_async_remote_copy(
            src_ref=bv.at[core], dst_ref=bv.at[core], send_sem=w_send.at[2], recv_sem=w_recv.at[2],
            device_id=partner, device_id_type=MESH,
        )

    def weight_copy(p):
        return pltpu.make_async_remote_copy(
            src_ref=weights.at[0, :, :, pl.ds(C * p, C), :], dst_ref=wv.at[core, :, :, pl.ds(C * p, C), :],
            send_sem=w_send.at[p], recv_sem=w_recv.at[p], device_id=partner, device_id_type=MESH,
        )

    cols48 = pl.multiple_of(32 * core, 16)
    to48 = pl.multiple_of(16 * (1 - core), 16)
    cols16 = pl.multiple_of(64 * core, 16)
    to16 = pl.multiple_of(48 * (1 - core), 16)

    def frame_copies(t):
        n = TOP - t

        def copy(kind, from_row, to_row, count, wide, target):
            src = fyb.at[t, pl.ds(from_row, count), pl.ds(cols48, WIDE) if wide else pl.ds(cols16, 16)]
            dst = hb.at[t, pl.ds(to_row, count), pl.ds(to48, WIDE) if wide else pl.ds(to16, 16)]
            return pltpu.make_async_remote_copy(
                src_ref=src, dst_ref=dst, send_sem=fr_send.at[t, kind], recv_sem=fr_recv.at[t, kind],
                device_id=target, device_id_type=MESH,
            )

        return [
            (has_side & has_s, has_side & has_n, copy(3, CY - n, TOP - n, n, False, at(0, 1 - core, tile + side + TCOLS))),
            (has_side & has_n, has_side & has_s, copy(4, 0, TOP + CY, n, False, at(0, 1 - core, tile + side - TCOLS))),
            (has_s, has_n, copy(0, CY - n, TOP - n, n, True, at(0, core, tile + TCOLS))),
            (has_n, has_s, copy(1, 0, TOP + CY, n, True, at(0, core, tile - TCOLS))),
            (has_side, has_side, copy(2, 0, TOP, CY, False, at(0, 1 - core, tile + side))),
        ]

    def stage_copies(t, receiving=False):
        k = TIME - 1 - t

        def copy(kind, from_row, to_row, count, target, lands=None):
            lands = kind if receiving or lands is None else lands
            return pltpu.make_async_remote_copy(
                src_ref=zh.at[1, t, 1, pl.ds((TOP + from_row) * WIDE, count * WIDE)],
                dst_ref=hz.at[t, pl.ds(pl.multiple_of((TOP + to_row) * WIDE, WIDE), count * WIDE)],
                send_sem=z_send.at[t, kind], recv_sem=z_recv.at[t, lands], device_id=target, device_id_type=MESH,
            )

        unread = CY + TOP
        return [
            copy(
                0, CY - 2 - k, jnp.where(has_s, -2 - k, unread), 2, at(1, core, jnp.where(has_s, tile + TCOLS, tile)),
                jnp.where(has_s, 0, 1),
            ),
            copy(
                1, k, jnp.where(has_n, CY + k, unread), 2, at(1, core, jnp.where(has_n, tile - TCOLS, tile)),
                jnp.where(has_n, 1, 0),
            ),
            *[copy(2 + i, y, y, count, at(1, core, tile)) for i, (y, count) in enumerate(OWN[t])],
        ]

    def put_input(t, rows, width, first_column, low=0, count=None):
        target = zin0 if width == FIRST else zin.at[t]
        count = width if count is None else count
        for y in rows:
            for b in range(3):
                begin = y * IW + first_column + low + b - 1
                target[b, y * width + low : y * width + low + count, :] = fin[t, begin : begin + count, :].astype(BF)

    def frame_width(t):
        return (FIRST, 12) if t == 0 else (WIDE, 20)

    own_rows = range(TOP, TOP + CY)

    def await_frame(t):
        for _, gets, cp in frame_copies(t):
            pl.when(gets)(cp.wait_recv)

    def get_frame(t):
        halo_rows = [*range(t, TOP), *range(TOP + CY, ROWS - t)]
        width, first_column = frame_width(t)
        for y in halo_rows:
            fin[t, pl.ds(pl.multiple_of(y * IW + 8 + 8 * core, 8), FIRST), :] = hb[t, y].astype(F32)
        for y in own_rows:
            fin[t, pl.ds(pl.multiple_of(y * IW + 8 + 56 * core, 8), 16), :] = hb[
                t, y, pl.ds(pl.multiple_of(48 * core, 16), 16), :
            ].astype(F32)
        put_input(t, halo_rows, width, first_column)
        put_input(t, own_rows, width, first_column, 0, 16)
        put_input(t, own_rows, width, first_column, width - 16, 16)

    def get_hidden(t):
        k = TIME - 1 - t
        copies = stage_copies(t, receiving=True)
        parts = [(copies[2 + i : 3 + i], range(y, y + count)) for i, (y, count) in enumerate(OWN[t])]
        parts.append((copies[:2], [-2 - k, -1 - k, CY + k, CY + k + 1]))
        for waits, lines in parts:
            for cp in waits:
                cp.wait_recv()
            rows = [TOP + line for line in lines]
            for y in rows:
                fin[t, y * IW + 24 : y * IW + 24 + WIDE, :] = hz[t, y * WIDE : (y + 1) * WIDE, :].astype(F32)
            put_input(t, rows, WIDE, 24)

    @pl.when(first_stage)
    def _():
        @pl.when(jnp.logical_not(has_n & has_s & has_side))
        def _():
            hb[...] = jnp.zeros_like(hb)

    @pl.when(jnp.logical_not(first_stage))
    def _():
        hz[...] = jnp.zeros_like(hz)

    barrier = pltpu.get_barrier_semaphore()

    def greet(device):
        pl.semaphore_signal(barrier, inc=1, device_id=device, device_id_type=MESH)

    @pl.when(first_stage)
    def _():
        pl.when(has_side & has_n)(lambda: greet(at(0, 1 - core, tile + side - TCOLS)))
        pl.when(has_side & has_s)(lambda: greet(at(0, 1 - core, tile + side + TCOLS)))
        pl.when(has_side)(lambda: greet(at(0, 1 - core, tile + side)))
        pl.when(has_n)(lambda: greet(at(0, core, tile - TCOLS)))
        pl.when(has_s)(lambda: greet(at(0, core, tile + TCOLS)))

    pl.when(has_n)(lambda: greet(at(1 - stage, core, tile - TCOLS)))
    pl.when(has_s)(lambda: greet(at(1 - stage, core, tile + TCOLS)))
    greet(at(1 - stage, core, tile))
    greet(partner)

    def put_rows(t):
        for x in range(CX):
            s32[CY * x : CY * (x + 1), :] = fr[t, :, C * x : C * (x + 1)].astype(F32)
        for y in range(CY):
            fyb[t, y] = s32[pl.ds(y, CX, stride=CY), :].astype(BF)

    def send_frame(t):
        for sends, _, cp in frame_copies(t):
            pl.when(sends)(cp.start)

    bv[core] = jnp.broadcast_to(bias[...].astype(F32), (8, 4 * C))

    @pl.when(first_stage)
    def _():
        load_f.wait()
        put_rows(0)

    one = lambda c: c.astype(jnp.int32)
    near = one(has_n) + one(has_s)
    mine = 2 + near
    tiles = near + one(has_side) + one(has_side & has_n) + one(has_side & has_s)
    pl.semaphore_wait(barrier, mine + jnp.where(first_stage, tiles, 0))

    @pl.when(first_stage)
    def _():
        send_frame(0)

    bias_copy().start()
    weight_copy(0).start()

    @pl.when(first_stage)
    def _():
        put_rows(1)
        send_frame(1)
        put_rows(2)
        send_frame(2)

    weight_copy(1).start()

    hid[...] = jnp.zeros_like(hid)
    fin[...] = jnp.zeros_like(fin)

    @pl.when(first_stage)
    def _():
        for t in range(TIME):
            for y in range(CY):
                fin[t, pl.ds(pl.multiple_of((y + TOP) * IW + 24 - 8 * core, 8), WIDE), :] = fyb[
                    t, y, pl.ds(cols48, WIDE), :
                ].astype(F32)
            width, first_column = frame_width(t)
            put_input(t, own_rows, width, first_column, 16, width - 32)

    def column_mask(width, first):
        x = lax.broadcasted_iota(jnp.int32, (width, C), 0) + (first + HALF * core + CX * col)
        return (x >= 0) & (x < CX * TCOLS)

    masks = {WIDE: column_mask(WIDE, -4), FIRST: column_mask(FIRST, -12)}

    def taps(groups, width, array):
        pieces = []
        for a in range(3):
            for b in range(3):
                rows = [array[b, pl.ds((y + a - 1 + TOP) * width, count * width), :] for y, count in groups]
                pieces.append(rows[0] if len(rows) == 1 else jnp.concatenate(rows, axis=0))
        return jnp.concatenate(pieces, axis=1)

    def all_rows(layer, t):
        y = -((1 - layer) + (TIME - 1 - t))
        chunks = []
        for count in CHUNKS[layer][CY - 2 * y]:
            chunks.append([(y, count)])
            y += count
        return chunks

    parts = (part0, part1)

    def hidden_part(layer, t):
        k = (1 - layer) + (TIME - 1 - t)
        for groups in all_rows(layer, t):
            ((y, count),) = groups
            parts[layer][(y + k) * WIDE : (y + k + count) * WIDE, :] = jnp.dot(
                taps(groups, WIDE, zh.at[layer, t - 1]),
                wv[layer, :, :, C:, :].reshape(9 * C, 4 * C),
                preferred_element_type=F32,
            )

    def step(layer, t, width=WIDE, split=False, chunks=None):
        k = (1 - layer) + (TIME - 1 - t)
        split = split and t > 0
        whole = t > 0 and not split
        source = zh.at[0, t] if layer == 1 else (zin0 if width == FIRST else zin.at[t])

        def chunk(groups):
            columns = taps(groups, width, source)
            factors = wv[layer, :, :, :C, :].reshape(9 * C, 4 * C)
            if whole:
                columns = jnp.concatenate([taps(groups, width, zh.at[layer, t - 1]), columns], axis=1)
                factors = jnp.concatenate([wv[layer, :, :, C:, :].reshape(9 * C, 4 * C), factors], axis=0)
            gates = jnp.dot(columns, factors, preferred_element_type=F32) + bv[layer, 0:1, :]
            if split:
                gates = gates + parts[layer][(groups[0][0] + k) * WIDE : (groups[0][0] + k + groups[0][1]) * WIDE, :]
            c_new = sigmoid(gates[:, :C]) * jnp.tanh(gates[:, 3 * C :])
            if t > 0:
                old = [cell[layer, pl.ds((y + TOP) * WIDE, count * WIDE), :] for y, count in groups]
                old = old[0] if len(old) == 1 else jnp.concatenate(old, axis=0)
                c_new = sigmoid(gates[:, C : 2 * C]) * old + c_new
            h_new = sigmoid(gates[:, 2 * C : 3 * C]) * jnp.tanh(c_new)
            lines = [y + i for y, count in groups for i in range(count)]
            for i, line in enumerate(lines):
                inside = masks[width]
                if line < 0:
                    inside = inside & has_n
                if line >= CY:
                    inside = inside & has_s
                h_row = jnp.where(inside, h_new[i * width : (i + 1) * width, :], 0.0)
                begin = (line + TOP) * FW + 16
                edge = (width - WIDE) // 2
                hid[layer, t, begin - edge : begin + WIDE + edge, :] = h_row
                cell[layer, (line + TOP) * WIDE : (line + TOP + 1) * WIDE, :] = c_new[
                    i * width + edge : (i + 1) * width - edge, :
                ]
                for b in range(3):
                    zh[layer, t, b, (line + TOP) * WIDE : (line + TOP + 1) * WIDE, :] = hid[
                        layer, t, begin + b - 1 : begin + b - 1 + WIDE, :
                    ].astype(BF)

        return [functools.partial(chunk, groups) for groups in chunks or all_rows(layer, t)]

    begin = pl.multiple_of(core * (HALF * C), C)
    half = pl.ds(begin, HALF * C)

    def give(slot, src, dst):
        return pltpu.make_async_remote_copy(
            src_ref=src, dst_ref=dst, send_sem=o_send.at[slot], recv_sem=o_recv.at[slot],
            device_id=partner, device_id_type=MESH,
        )

    def give_hidden(t):
        return give(t, hs.at[t], out_h.at[0, t, 0, :, half])

    def give_cell():
        return give(TIME, cs, out_c.at[0, 0, :, half])

    def hidden_of(layer, t, x):
        return hid[layer, t, pl.ds(TOP * FW + 20 + x, CY, stride=FW), :].astype(BF)

    def cell_of(layer, x):
        return cell[layer, pl.ds(TOP * WIDE + 4 + x, CY, stride=WIDE), :]

    def put_hidden(layer, t):
        @pl.when(core == layer)
        def _():
            for x in range(HALF):
                out_h[0, t, 0, :, pl.ds(pl.multiple_of(begin + C * x, C), C)] = hidden_of(layer, t, x)

        @pl.when(core != layer)
        def _():
            for x in range(HALF):
                hs[t, :, C * x : C * (x + 1)] = hidden_of(layer, t, x)
            give_hidden(t).start()

    def put_cell(layer):
        @pl.when(core == layer)
        def _():
            for x in range(HALF):
                out_c[0, 0, :, pl.ds(pl.multiple_of(begin + C * x, C), C)] = cell_of(layer, x)

        @pl.when(core != layer)
        def _():
            for x in range(HALF):
                cs[:, C * x : C * (x + 1)] = cell_of(layer, x)
            give_cell().start()

    for p in range(2):
        own_w[p].wait()

    def get_weights(t):
        if t == 0:
            bias_copy().wait_recv()
            weight_copy(0).wait_recv()
        if t == 1:
            weight_copy(1).wait_recv()

    @pl.when(first_stage)
    def _():
        orders = (
            ([[(-3, 4)], [(1, 3)], [(4, 3)], [(7, 4)]], [[(-2, 4)], [(2, 4)], [(6, 4)]], "aabSabSabS", ((2,), (1, 0, 3), (4,))),
            ([[(-2, 4)], [(2, 4)], [(6, 4)]], [[(-1, 4)], [(3, 3)], [(6, 3)]], "aabSabSbS", ((1, 2), (3,), (0, 4))),
            ([[(-1, 4)], [(5, 4)], [(3, 2)]], [[(0, 2), (6, 2)], [(2, 4)]], "aabSabS", ((1, 0, 2, 3), (4,))),
        )
        for t in range(TIME):
            await_frame(t)
            get_weights(t)
            get_frame(t)
            lower, upper, order, kinds = orders[t]
            lower = iter(step(0, t, FIRST if t == 0 else WIDE, chunks=lower))
            upper = iter(step(1, t, chunks=upper))
            kinds = iter(kinds)
            copies = stage_copies(t)
            for what in order:
                if what == "a":
                    next(lower)()
                elif what == "b":
                    next(upper)()
                else:
                    for kind in next(kinds):
                        copies[kind].start()
        for t in range(TIME):
            for layer in range(2):
                put_hidden(layer, t)
        for layer in range(2):
            put_cell(layer)

    @pl.when(jnp.logical_not(first_stage))
    def _():
        for t in range(TIME):
            get_weights(t)
            if t > 0:
                hidden_part(0, t)
                hidden_part(1, t)
            get_hidden(t)
            for chunk in step(0, t, split=True):
                chunk()
            put_hidden(0, t)
            if t == TIME - 1:
                put_cell(0)
            for chunk in step(1, t, split=True):
                chunk()
            put_hidden(1, t)
        put_cell(1)

    bias_copy().wait_send()
    for p in range(2):
        weight_copy(p).wait_send()

    @pl.when(first_stage)
    def _():
        for t in range(TIME):
            for sends, _, cp in frame_copies(t):
                pl.when(sends)(cp.wait_send)
            for cp in stage_copies(t):
                cp.wait_send()

    for t in range(TIME):
        give_hidden(t).wait()
    give_cell().wait()


def local(frames, weights, bias):
    vmem = pl.BlockSpec(memory_space=pltpu.VMEM)
    hbm = pl.BlockSpec(memory_space=pltpu.HBM)
    dma = pltpu.SemaphoreType.DMA
    return pl.pallas_call(
        kernel,
        out_shape=(
            pltpu.VMEM((1, TIME, 1, CY, CX * C), BF),
            pltpu.VMEM((1, 1, CY, CX * C), F32),
        ),
        in_specs=[hbm, hbm, vmem],
        out_specs=(vmem, vmem),
        scratch_shapes=[
            pltpu.VMEM((TIME, CY, CX * C), BF),
            pltpu.VMEM((CY * CX, C), F32),
            pltpu.VMEM((TIME, CY, CX, C), BF),
            pltpu.VMEM((TIME, ROWS, FIRST, C), BF),
            pltpu.VMEM((TIME, (ROWS + 2) * WIDE, C), BF),
            pltpu.VMEM((TIME, ROWS * IW, C), F32),
            pltpu.VMEM((3, ROWS * FIRST, C), BF),
            pltpu.VMEM((TIME, 3, ROWS * WIDE, C), BF),
            pltpu.VMEM((2, TIME, 3, ROWS * WIDE, C), BF),
            pltpu.VMEM((2, TIME, ROWS * FW, C), F32),
            pltpu.VMEM((2, ROWS * WIDE, C), F32),
            pltpu.VMEM(((CY + 4) * WIDE, 4 * C), F32),
            pltpu.VMEM(((CY + 2) * WIDE, 4 * C), F32),
            pltpu.VMEM((2, 3, 3, 2 * C, 4 * C), BF),
            pltpu.VMEM((2, 8, 4 * C), F32),
            pltpu.VMEM((TIME, CY, HALF * C), BF),
            pltpu.VMEM((CY, HALF * C), F32),
            dma((12,)),
            dma((3,)),
            dma((3,)),
            dma((TIME, 5)),
            dma((TIME, 5)),
            dma((TIME, 5)),
            dma((TIME, 5)),
            dma((TIME + 1,)),
            dma((TIME + 1,)),
        ],
        compiler_params=pltpu.CompilerParams(
            collective_id=0, has_side_effects=True, vmem_limit_bytes=58 * 2**20
        ),
    )(frames, weights, bias)


def solution(mesh):
    return jax.shard_map(
        local,
        mesh=mesh,
        in_specs=(P(None, "tile", None, None), P("section", None, None, None, None), P("section", None)),
        out_specs=(P("section", None, "tile", None, None), P("section", "tile", None, None)),
        check_vma=False,
    )
```

time: 39.7 us -> 35.6 us (0.90)
  local copies, waits for them, and re-layouts: 4.87 us -> 1.5 us
  Pallas kernels: 34 us -> 33.2 us
    unnamed x8 -> x2, local copies, waits for them, and re-layouts: 4.87 us -> 1.5 us
    pallas_call x1, Pallas kernels: 34 us -> 33.2 us  [local(): pl.pallas_call(kernel, out_shape=(pltpu.VMEM((1, TIME, 1, CY, CX * C), BF...]
where the time goes in v2:
time: 35.6 us; the launch traced here: 35.4 us
  Pallas kernels  33.2 us (93%)
  local copies, waits for them, and re-layouts  1.5 us (4%)
  between operations  0.64 us (2%)
    pallas_call x1, Pallas kernels, local(): pl.pallas_call(kernel, out_shape=(pltpu.VMEM((1, TIME, 1, CY, CX * C), BF...  33.2 us
    unnamed x2, local copies, waits for them, and re-layouts  1.5 us

profile of v2, /device:TPU:43, one launch (start us, length us, event | category | flops | bytes accessed | tf_op | source)
XLA Modules:
  0.0 35.4 jit_solution(13829557348257435036)
XLA Ops:
  0.6 33.2 %shard_map.50 = (bf16[1,3,1,8,10240]{4,3,2,1,0:T(8,128)(2,1)S(1)}, f32[1,1,8,10240]{3,2,1,0:T(8,128)S(1)}) custom-call(bf16[3,1,8,10240]{3,2,1,0:T(8,128)(2,1)} %frames.1, bf16[1,3,3,256,512]{4,3,2,1,0:T(8,128)(2,1)} %weights.1, bf16[1,512]{1,0:T(2,128)(2,1)} %bias.1), custom_call_target="tpu_custom_call" | custom-call | tf_op jit(solution)/shard_map/pallas_call | solution.py:446
  33.9 0.8 %copy.7 = bf16[1,3,1,8,10240]{4,3,2,1,0:T(8,128)(2,1)} copy(bf16[1,3,1,8,10240]{4,3,2,1,0:T(8,128)(2,1)S(1)} %get-tuple-element.2) | data formatting | bytes 983040
  34.6 0.7 %copy.8 = f32[1,1,8,10240]{3,2,1,0:T(8,128)} copy(f32[1,1,8,10240]{3,2,1,0:T(8,128)S(1)} %get-tuple-element.3) | data formatting | bytes 655360

commit v3 on v2

--- a/solution.py
+++ b/solution.py
@@ -150,12 +150,13 @@
         put_input(t, own_rows, width, first_column, 0, 16)
         put_input(t, own_rows, width, first_column, width - 16, 16)
 
-    def get_hidden(t):
+    def get_hidden(t, pieces):
         k = TIME - 1 - t
         copies = stage_copies(t, receiving=True)
         parts = [(copies[2 + i : 3 + i], range(y, y + count)) for i, (y, count) in enumerate(OWN[t])]
         parts.append((copies[:2], [-2 - k, -1 - k, CY + k, CY + k + 1]))
-        for waits, lines in parts:
+        for piece in pieces:
+            waits, lines = parts[piece]
             for cp in waits:
                 cp.wait_recv()
             rows = [TOP + line for line in lines]
@@ -319,50 +320,31 @@
 
         return [functools.partial(chunk, groups) for groups in chunks or all_rows(layer, t)]
 
-    begin = pl.multiple_of(core * (HALF * C), C)
-    half = pl.ds(begin, HALF * C)
+    half = pl.ds(pl.multiple_of(core * (HALF * C), C), HALF * C)
+
+    def keep(slot, src, dst):
+        return pltpu.make_async_copy(src.at[core], dst, local_sem.at[8 + slot])
 
     def give(slot, src, dst):
         return pltpu.make_async_remote_copy(
-            src_ref=src, dst_ref=dst, send_sem=o_send.at[slot], recv_sem=o_recv.at[slot],
+            src_ref=src.at[1 - core], dst_ref=dst, send_sem=o_send.at[slot], recv_sem=o_recv.at[slot],
             device_id=partner, device_id_type=MESH,
         )
 
-    def give_hidden(t):
-        return give(t, hs.at[t], out_h.at[0, t, 0, :, half])
-
-    def give_cell():
-        return give(TIME, cs, out_c.at[0, 0, :, half])
-
-    def hidden_of(layer, t, x):
-        return hid[layer, t, pl.ds(TOP * FW + 20 + x, CY, stride=FW), :].astype(BF)
-
-    def cell_of(layer, x):
-        return cell[layer, pl.ds(TOP * WIDE + 4 + x, CY, stride=WIDE), :]
+    def hidden_result(t):
+        return t, hs.at[:, t], out_h.at[0, t, 0, :, half]
+
+    cell_result = TIME, cs, out_c.at[0, 0, :, half]
 
     def put_hidden(layer, t):
-        @pl.when(core == layer)
-        def _():
-            for x in range(HALF):
-                out_h[0, t, 0, :, pl.ds(pl.multiple_of(begin + C * x, C), C)] = hidden_of(layer, t, x)
-
-        @pl.when(core != layer)
-        def _():
-            for x in range(HALF):
-                hs[t, :, C * x : C * (x + 1)] = hidden_of(layer, t, x)
-            give_hidden(t).start()
+        for x in range(HALF):
+            hs[layer, t, :, C * x : C * (x + 1)] = hid[
+                layer, t, pl.ds(TOP * FW + 20 + x, CY, stride=FW), :
+            ].astype(BF)
 
     def put_cell(layer):
-        @pl.when(core == layer)
-        def _():
-            for x in range(HALF):
-                out_c[0, 0, :, pl.ds(pl.multiple_of(begin + C * x, C), C)] = cell_of(layer, x)
-
-        @pl.when(core != layer)
-        def _():
-            for x in range(HALF):
-                cs[:, C * x : C * (x + 1)] = cell_of(layer, x)
-            give_cell().start()
+        for x in range(HALF):
+            cs[layer, :, C * x : C * (x + 1)] = cell[layer, pl.ds(TOP * WIDE + 4 + x, CY, stride=WIDE), :]
 
     for p in range(2):
         own_w[p].wait()
@@ -378,7 +360,7 @@
     def _():
         orders = (
             ([[(-3, 4)], [(1, 3)], [(4, 3)], [(7, 4)]], [[(-2, 4)], [(2, 4)], [(6, 4)]], "aabSabSabS", ((2,), (1, 0, 3), (4,))),
-            ([[(-2, 4)], [(2, 4)], [(6, 4)]], [[(-1, 4)], [(3, 3)], [(6, 3)]], "aabSabSbS", ((1, 2), (3,), (0, 4))),
+            ([[(0, 4)], [(4, 4)], [(-2, 2), (8, 2)]], [[(1, 2), (5, 2)], [(-1, 2), (3, 2), (7, 2)]], "aabSabS", ((1, 0), (2, 3, 4))),
             ([[(-1, 4)], [(5, 4)], [(3, 2)]], [[(0, 2), (6, 2)], [(2, 4)]], "aabSabS", ((1, 0, 2, 3), (4,))),
         )
         for t in range(TIME):
@@ -401,26 +383,52 @@
         for t in range(TIME):
             for layer in range(2):
                 put_hidden(layer, t)
+            give(*hidden_result(t)).start()
+            keep(*hidden_result(t)).start()
         for layer in range(2):
             put_cell(layer)
+        give(*cell_result).start()
+        keep(*cell_result).start()
 
     @pl.when(jnp.logical_not(first_stage))
     def _():
         for t in range(TIME):
             get_weights(t)
-            if t > 0:
+            if t == 0:
+                get_hidden(0, (0, 1))
+                chunks = iter(step(0, 0, chunks=[[(1, 3)], [(4, 3)], [(-3, 4)], [(7, 4)]]))
+                next(chunks)()
+                get_hidden(0, (2,))
+                next(chunks)()
+                get_hidden(0, (3,))
+            else:
                 hidden_part(0, t)
                 hidden_part(1, t)
-            get_hidden(t)
-            for chunk in step(0, t, split=True):
+                get_hidden(t, (0, 1, 2, 3))
+                chunks = step(0, t, split=True)
+            for chunk in chunks:
                 chunk()
-            put_hidden(0, t)
-            if t == TIME - 1:
-                put_cell(0)
-            for chunk in step(1, t, split=True):
-                chunk()
-            put_hidden(1, t)
+            if t < TIME - 1:
+                for chunk in step(1, t, split=True):
+                    chunk()
+                put_hidden(0, t)
+                put_hidden(1, t)
+                give(*hidden_result(t)).start()
+                keep(*hidden_result(t)).start()
+        t = TIME - 1
+        upper, lower = step(1, t, split=True)
+        upper()
+        put_hidden(0, t)
+        put_cell(0)
+        for result in (hidden_result(t), cell_result):
+            pl.when(core == 1)(give(*result).start)
+            pl.when(core == 0)(keep(*result).start)
+        lower()
+        put_hidden(1, t)
         put_cell(1)
+        for result in (hidden_result(t), cell_result):
+            pl.when(core == 0)(give(*result).start)
+            pl.when(core == 1)(keep(*result).start)
 
     bias_copy().wait_send()
     for p in range(2):
@@ -434,9 +442,9 @@
             for cp in stage_copies(t):
                 cp.wait_send()
 
-    for t in range(TIME):
-        give_hidden(t).wait()
-    give_cell().wait()
+    for result in (*[hidden_result(t) for t in range(TIME)], cell_result):
+        keep(*result).wait()
+        give(*result).wait()
 
 
 def local(frames, weights, bias):
@@ -467,8 +475,8 @@
             pltpu.VMEM(((CY + 2) * WIDE, 4 * C), F32),
             pltpu.VMEM((2, 3, 3, 2 * C, 4 * C), BF),
             pltpu.VMEM((2, 8, 4 * C), F32),
-            pltpu.VMEM((TIME, CY, HALF * C), BF),
-            pltpu.VMEM((CY, HALF * C), F32),
+            pltpu.VMEM((2, TIME, CY, HALF * C), BF),
+            pltpu.VMEM((2, CY, HALF * C), F32),
             dma((12,)),
             dma((3,)),
             dma((3,)),

time: 35.6 us -> 34.5 us (0.969)
  Pallas kernels: 33.2 us -> 32.2 us
    pallas_call x1, Pallas kernels: 33.2 us -> 32.2 us  [local(): pl.pallas_call(kernel, out_shape=(pltpu.VMEM((1, TIME, 1, CY, CX * C), BF...]
where the time goes in v3:
time: 34.5 us; the launch traced here: 34.3 us
  Pallas kernels  32.2 us (93%)
  local copies, waits for them, and re-layouts  1.5 us (4%)
  between operations  0.64 us (2%)
    pallas_call x1, Pallas kernels, local(): pl.pallas_call(kernel, out_shape=(pltpu.VMEM((1, TIME, 1, CY, CX * C), BF...  32.2 us
    unnamed x2, local copies, waits for them, and re-layouts  1.5 us

profile of v3, /device:TPU:43, one launch (start us, length us, event | category | flops | bytes accessed | tf_op | source)
XLA Modules:
  0.0 34.3 jit_solution(11727141802896289134)
XLA Ops:
  0.6 32.2 %shard_map.50 = (bf16[1,3,1,8,10240]{4,3,2,1,0:T(8,128)(2,1)S(1)}, f32[1,1,8,10240]{3,2,1,0:T(8,128)S(1)}) custom-call(bf16[3,1,8,10240]{3,2,1,0:T(8,128)(2,1)} %frames.1, bf16[1,3,3,256,512]{4,3,2,1,0:T(8,128)(2,1)} %weights.1, bf16[1,512]{1,0:T(2,128)(2,1)} %bias.1), custom_call_target="tpu_custom_call" | custom-call | tf_op jit(solution)/shard_map/pallas_call | solution.py:454
  32.8 0.8 %copy.7 = bf16[1,3,1,8,10240]{4,3,2,1,0:T(8,128)(2,1)} copy(bf16[1,3,1,8,10240]{4,3,2,1,0:T(8,128)(2,1)S(1)} %get-tuple-element.2) | data formatting | bytes 983040
  33.6 0.7 %copy.8 = f32[1,1,8,10240]{3,2,1,0:T(8,128)} copy(f32[1,1,8,10240]{3,2,1,0:T(8,128)S(1)} %get-tuple-element.3) | data formatting | bytes 655360

commit v4 on v3

--- a/solution.py
+++ b/solution.py
@@ -91,9 +91,9 @@
         return [
             (has_side & has_s, has_side & has_n, copy(3, CY - n, TOP - n, n, False, at(0, 1 - core, tile + side + TCOLS))),
             (has_side & has_n, has_side & has_s, copy(4, 0, TOP + CY, n, False, at(0, 1 - core, tile + side - TCOLS))),
+            (has_side, has_side, copy(2, 0, TOP, CY, False, at(0, 1 - core, tile + side))),
             (has_s, has_n, copy(0, CY - n, TOP - n, n, True, at(0, core, tile + TCOLS))),
             (has_n, has_s, copy(1, 0, TOP + CY, n, True, at(0, core, tile - TCOLS))),
-            (has_side, has_side, copy(2, 0, TOP, CY, False, at(0, 1 - core, tile + side))),
         ]
 
     def stage_copies(t, receiving=False):
@@ -133,22 +133,26 @@
 
     own_rows = range(TOP, TOP + CY)
 
-    def await_frame(t):
-        for _, gets, cp in frame_copies(t):
+    def get_side(t):
+        _, gets, cp = frame_copies(t)[2]
+        pl.when(gets)(cp.wait_recv)
+        width, first_column = frame_width(t)
+        for y in own_rows:
+            fin[t, pl.ds(pl.multiple_of(y * IW + 8 + 56 * core, 8), 16), :] = hb[
+                t, y, pl.ds(pl.multiple_of(48 * core, 16), 16), :
+            ].astype(F32)
+        put_input(t, own_rows, width, first_column, 0, 16)
+        put_input(t, own_rows, width, first_column, width - 16, 16)
+
+    def get_rows(t):
+        copies = frame_copies(t)
+        for _, gets, cp in copies[:2] + copies[3:]:
             pl.when(gets)(cp.wait_recv)
-
-    def get_frame(t):
         halo_rows = [*range(t, TOP), *range(TOP + CY, ROWS - t)]
         width, first_column = frame_width(t)
         for y in halo_rows:
             fin[t, pl.ds(pl.multiple_of(y * IW + 8 + 8 * core, 8), FIRST), :] = hb[t, y].astype(F32)
-        for y in own_rows:
-            fin[t, pl.ds(pl.multiple_of(y * IW + 8 + 56 * core, 8), 16), :] = hb[
-                t, y, pl.ds(pl.multiple_of(48 * core, 16), 16), :
-            ].astype(F32)
         put_input(t, halo_rows, width, first_column)
-        put_input(t, own_rows, width, first_column, 0, 16)
-        put_input(t, own_rows, width, first_column, width - 16, 16)
 
     def get_hidden(t, pieces):
         k = TIME - 1 - t
@@ -359,14 +363,13 @@
     @pl.when(first_stage)
     def _():
         orders = (
-            ([[(-3, 4)], [(1, 3)], [(4, 3)], [(7, 4)]], [[(-2, 4)], [(2, 4)], [(6, 4)]], "aabSabSabS", ((2,), (1, 0, 3), (4,))),
-            ([[(0, 4)], [(4, 4)], [(-2, 2), (8, 2)]], [[(1, 2), (5, 2)], [(-1, 2), (3, 2), (7, 2)]], "aabSabS", ((1, 0), (2, 3, 4))),
-            ([[(-1, 4)], [(5, 4)], [(3, 2)]], [[(0, 2), (6, 2)], [(2, 4)]], "aabSabS", ((1, 0, 2, 3), (4,))),
+            ([[(1, 3)], [(4, 3)], [(-3, 4)], [(7, 4)]], [[(2, 4)], [(-2, 4)], [(6, 4)]], "aabSRaabSbS", ((1, 0, 3), (2,), (4,))),
+            ([[(0, 4)], [(4, 4)], [(-2, 2), (8, 2)]], [[(1, 2), (5, 2)], [(-1, 2), (3, 2), (7, 2)]], "RaabSabS", ((1, 0), (2, 3, 4))),
+            ([[(-1, 4)], [(5, 4)], [(3, 2)]], [[(0, 2), (6, 2)], [(2, 4)]], "RaabSabS", ((1, 0, 2, 3), (4,))),
         )
         for t in range(TIME):
-            await_frame(t)
             get_weights(t)
-            get_frame(t)
+            get_side(t)
             lower, upper, order, kinds = orders[t]
             lower = iter(step(0, t, FIRST if t == 0 else WIDE, chunks=lower))
             upper = iter(step(1, t, chunks=upper))
@@ -377,6 +380,8 @@
                     next(lower)()
                 elif what == "b":
                     next(upper)()
+                elif what == "R":
+                    get_rows(t)
                 else:
                     for kind in next(kinds):
                         copies[kind].start()

time: 34.5 us -> 32.8 us (0.951)
  Pallas kernels: 32.2 us -> 30.5 us
    pallas_call x1, Pallas kernels: 32.2 us -> 30.5 us  [local(): pl.pallas_call(kernel, out_shape=(pltpu.VMEM((1, TIME, 1, CY, CX * C), BF...]
where the time goes in v4:
time: 32.8 us; the launch traced here: 32.7 us
  Pallas kernels  30.5 us (93%)
  local copies, waits for them, and re-layouts  1.5 us (5%)
  between operations  0.64 us (2%)
    pallas_call x1, Pallas kernels, local(): pl.pallas_call(kernel, out_shape=(pltpu.VMEM((1, TIME, 1, CY, CX * C), BF...  30.5 us
    unnamed x2, local copies, waits for them, and re-layouts  1.5 us

profile of v4, /device:TPU:43, one launch (start us, length us, event | category | flops | bytes accessed | tf_op | source)
XLA Modules:
  0.0 32.7 jit_solution(5491149859473058754)
XLA Ops:
  0.6 30.5 %shard_map.50 = (bf16[1,3,1,8,10240]{4,3,2,1,0:T(8,128)(2,1)S(1)}, f32[1,1,8,10240]{3,2,1,0:T(8,128)S(1)}) custom-call(bf16[3,1,8,10240]{3,2,1,0:T(8,128)(2,1)} %frames.1, bf16[1,3,3,256,512]{4,3,2,1,0:T(8,128)(2,1)} %weights.1, bf16[1,512]{1,0:T(2,128)(2,1)} %bias.1), custom_call_target="tpu_custom_call" | custom-call | tf_op jit(solution)/shard_map/pallas_call | solution.py:459
  31.2 0.8 %copy.7 = bf16[1,3,1,8,10240]{4,3,2,1,0:T(8,128)(2,1)} copy(bf16[1,3,1,8,10240]{4,3,2,1,0:T(8,128)(2,1)S(1)} %get-tuple-element.2) | data formatting | bytes 983040
  32.0 0.7 %copy.8 = f32[1,1,8,10240]{3,2,1,0:T(8,128)} copy(f32[1,1,8,10240]{3,2,1,0:T(8,128)S(1)} %get-tuple-element.3) | data formatting | bytes 655360
